TPU v7x, 512 devices: a whole 4x4x16 slice. The times are simulated.
512 devices in a mesh: fsdp: 32 (over x, z_lo, core), sp: 16 (over y, z_hi).
Axes of the slice: x: 4, y: 4, z: 16 (z_hi: 4, z_lo: 4; z = z_hi * 4 + z_lo), core: 2. Of those that a mesh axis runs over, the one named last changes fastest.
Arguments:
- query: bfloat16 [32, 2048, 4096], P('fsdp', 'sp'), may hold values from -6 to 6
- key: bfloat16 [32, 2048, 4096], P('fsdp', 'sp'), may hold values from -6 to 6
- value: bfloat16 [32, 2048, 4096], P('fsdp', 'sp'), may hold values from -6 to 6
- cotangent: bfloat16 [32, 2048, 4096], P('fsdp', 'sp')
- gain_q: float32 [32, 128], P('sp', 'fsdp'), may hold values from 0.5 to 5
- gain_k: float32 [32, 128], P('sp', 'fsdp'), may hold values from 0.5 to 5
- windows: int32 [16, 6], replicated, may hold values from 0 to 15, as said below
- order: int32 [2048], replicated, may hold values from 0 to 2047, as said below
Outputs:
- grad_gain_q: float32 [32, 128], P('sp', 'fsdp')
- grad_gain_k: float32 [32, 128], P('sp', 'fsdp')
Inputs may be any that keep to these rules, and one draw needn't show every extreme that they name: `windows`: row t lists 6 different tiles, the first of them t itself. `order`: each of the 2048 positions appears once.
All inputs are finite; a program needn't handle non-finite values.
Results may differ from a plain program's by a relative error of at most 0.0035.
The roundings to bfloat16 on the way count: a program that leaves them out, or rounds other values in their place, can miss the bound.
Values may be sent and summed in bfloat16 or wider, within the bound.
No kernel may reach another device: no remote copies, remote signals or barrier semaphores. Data moves between devices by JAX's collectives and lax.ppermute only.
A program may use at most 64 MiB of HBM per device.

v0:
```python
import jax
import jax.numpy as jnp
from jax import lax
from jax.sharding import PartitionSpec as P

TILE = 128


def normalize(rows, gain):
    wide = rows.astype(jnp.float32)
    unit = wide * lax.rsqrt(jnp.mean(wide * wide, axis=-1, keepdims=True) + 1e-06)
    return (unit, (unit * gain).astype(jnp.bfloat16))


def block_size(tiles, tile):
    group = max(1, min(tiles, 512 // tile))
    while tiles % group:
        group -= 1
    return group


def in_blocks(rows, group):
    return rows.reshape((rows.shape[0] // group, group) + rows.shape[1:])


def window_rows(rows, picks):
    taken = rows[picks]
    return taken.reshape(picks.shape[0], picks.shape[1] * rows.shape[1], rows.shape[2])


def block_scores(query_block, knorm, picks, scale):
    keys = window_rows(knorm, picks)
    scores = (
        jnp.einsum("tqd,tkd->tqk", query_block, keys, preferred_element_type=jnp.float32) * scale
    )
    return (keys, scores)


def head_forward(query_rows, key_rows, value_rows, gain_query, gain_key, windows, group):
    tiles, tile, width = query_rows.shape
    scale = width ** (-0.5)
    qhat, qnorm = normalize(query_rows, gain_query)
    khat, knorm = normalize(key_rows, gain_key)

    def one_block(items):
        query_block, picks = items
        keys, scores = block_scores(query_block, knorm, picks, scale)
        top = jnp.max(scores, axis=-1, keepdims=True)
        weights = jnp.exp(scores - top)
        total = jnp.sum(weights, axis=-1, keepdims=True)
        probs = weights / total
        values = window_rows(value_rows, picks)
        attended = jnp.einsum(
            "tqk,tkd->tqd", probs.astype(jnp.bfloat16), values, preferred_element_type=jnp.float32
        )
        return (top, total, attended)

    top, total, attended = lax.map(one_block, (in_blocks(qnorm, group), in_blocks(windows, group)))
    top = top.reshape(tiles, tile, 1)
    total = total.reshape(tiles, tile, 1)
    attended = attended.reshape(tiles, tile, width)
    return (qhat, khat, qnorm, knorm, value_rows, top, total, attended)


def head_backward(state, grad_rows, windows, group):
    qhat, khat, qnorm, knorm, value_rows, top, total, attended = state
    tiles, tile, width = qhat.shape
    count = windows.shape[1]
    scale = width ** (-0.5)
    rowterm = jnp.sum(grad_rows.astype(jnp.float32) * attended, axis=-1, keepdims=True)
    tile_ids = jnp.arange(tiles, dtype=jnp.int32)

    def one_block(dkey_rows, items):
        query_block, picks, top_block, total_block, term_block, grad_block = items
        keys, scores = block_scores(query_block, knorm, picks, scale)
        probs = jnp.exp(scores - top_block) / total_block
        values = window_rows(value_rows, picks)
        dprobs = jnp.einsum("tqd,tkd->tqk", grad_block, values, preferred_element_type=jnp.float32)
        dscores = (probs * (dprobs - term_block)).astype(jnp.bfloat16)
        dquery = (
            jnp.einsum("tqk,tkd->tqd", dscores, keys, preferred_element_type=jnp.float32) * scale
        )
        dkeys = (
            jnp.einsum("tqk,tqd->tkd", dscores, query_block, preferred_element_type=jnp.float32)
            * scale
        )
        dkeys = dkeys.reshape(picks.shape[0], count, tile, width)
        onehot = (picks[:, :, None] == tile_ids[None, None, :]).astype(jnp.float32)
        dkey_rows = dkey_rows + jnp.einsum(
            "tns,tnrd->srd", onehot, dkeys, precision=lax.Precision.HIGHEST
        )
        return (dkey_rows, dquery)

    start = jnp.zeros((tiles, tile, width), jnp.float32)
    items = (
        in_blocks(qnorm, group),
        in_blocks(windows, group),
        in_blocks(top, group),
        in_blocks(total, group),
        in_blocks(rowterm, group),
        in_blocks(grad_rows, group),
    )
    dkey_rows, dquery = lax.scan(one_block, start, items)
    dquery = dquery.reshape(tiles, tile, width)
    return (jnp.sum(dquery * qhat, axis=(0, 1)), jnp.sum(dkey_rows * khat, axis=(0, 1)))


def shards(query, key, value, cotangent, gain_q, gain_k, windows, order):
    groups = lax.axis_size("sp")
    tokens = query.shape[1]
    flat = query.shape[2]
    head_count = gain_q.shape[0]
    width = flat // (groups * head_count)
    group = block_size(tokens * groups // TILE, TILE)

    def split(rows):
        return rows.reshape(tokens, groups, flat // groups)

    def arrange(rows):
        rows = rows.reshape(-1, head_count, width)[order]
        tiles = rows.shape[0] // TILE
        return jnp.transpose(rows.reshape(tiles, TILE, head_count, width), (2, 0, 1, 3))

    gains_query, gains_key = (
        lax.all_gather(gain_q, "fsdp", axis=1, tiled=True),
        lax.all_gather(gain_k, "fsdp", axis=1, tiled=True),
    )
    query_here, key_here, value_here, grad_here = (
        lax.all_to_all(split(query), "sp", split_axis=1, concat_axis=0, tiled=True),
        lax.all_to_all(split(key), "sp", split_axis=1, concat_axis=0, tiled=True),
        lax.all_to_all(split(value), "sp", split_axis=1, concat_axis=0, tiled=True),
        lax.all_to_all(split(cotangent), "sp", split_axis=1, concat_axis=0, tiled=True),
    )

    def forward_one_head(items):
        return head_forward(items[0], items[1], items[2], items[3], items[4], windows, group)

    state = lax.map(
        forward_one_head,
        (arrange(query_here), arrange(key_here), arrange(value_here), gains_query, gains_key),
    )

    def backward_one_head(items):
        return head_backward(items[0], items[1], windows, group)

    terms_q, terms_k = lax.map(backward_one_head, (state, arrange(grad_here)))
    sums_q, sums_k = (
        lax.psum_scatter(terms_q, "fsdp", scatter_dimension=1, tiled=True),
        lax.psum_scatter(terms_k, "fsdp", scatter_dimension=1, tiled=True),
    )
    return (sums_q, sums_k)


def solution(mesh):
    placed = (
        P("fsdp", "sp", None),
        P("fsdp", "sp", None),
        P("fsdp", "sp", None),
        P("fsdp", "sp", None),
        P("sp", "fsdp"),
        P("sp", "fsdp"),
        P(),
        P(),
    )
    return jax.shard_map(
        shards,
        mesh=mesh,
        in_specs=placed,
        out_specs=(P("sp", "fsdp"), P("sp", "fsdp")),
        check_vma=False,
    )
```

profile of v0, /device:TPU:1, one launch (start us, length us, event | category | flops | bytes accessed | tf_op | source)
XLA Modules:
  0.0 570.7 jit_solution(3770852328568457459)
XLA Ops:
  2.9 18.5 %all-to-all-start.1 = ((bf16[128,16,256]{0,2,1:T(8,128)(2,1)}), bf16[128,16,256]{0,2,1:T(8,128)(2,1)S(1)}, u32[]{:S(2)}, u32[]{:S(2)}) async-start(bf16[128,16,256]{0,2,1:T(8,128)(2,1)} %bitcast.34), calls=%async_computation.1 | async-start | bytes 2097152 | tf_op jit(solution)/shard_map/all_to_all | solution.py:130
  22.8 48.1 %all-to-all-done.1 = bf16[128,16,256]{0,2,1:T(8,128)(2,1)S(1)} async-done(((bf16[128,16,256]{0,2,1:T(8,128)(2,1)}), bf16[128,16,256]{0,2,1:T(8,128)(2,1)S(1)}, u32[]{:S(2)}, u32[]{:S(2)}) %all-to-all-start.1) | async-done | bytes 1048608 | tf_op jit(solution)/shard_map/all_to_all | solution.py:130
  70.9 9.5 %all-to-all-start.2 = ((bf16[128,16,256]{0,2,1:T(8,128)(2,1)}), bf16[128,16,256]{0,2,1:T(8,128)(2,1)S(1)}, u32[]{:S(2)}, u32[]{:S(2)}) async-start(bf16[128,16,256]{0,2,1:T(8,128)(2,1)} %bitcast.45), calls=%async_computation.2 | async-start | bytes 2097152 | tf_op jit(solution)/shard_map/all_to_all | solution.py:131
  81.7 28.8 %all-to-all-done.2 = bf16[128,16,256]{0,2,1:T(8,128)(2,1)S(1)} async-done(((bf16[128,16,256]{0,2,1:T(8,128)(2,1)}), bf16[128,16,256]{0,2,1:T(8,128)(2,1)S(1)}, u32[]{:S(2)}, u32[]{:S(2)}) %all-to-all-start.2) | async-done | bytes 1048608 | tf_op jit(solution)/shard_map/all_to_all | solution.py:131
  110.5 4.1 all-to-all-start
  114.8 95.8 %all-gather = f32[32,4,2]{1,2,0:T(2,128)S(1)} all-gather(f32[1,4,2]{1,2,0:T(2,128)S(1)} %bitcast.293), channel_id=1, replica_groups=mesh['fsdp'=32,'sp'=16] {'fsdp'}, dimensions={0}, use_global_device_ids=true | all-gather | bytes 1056 | tf_op jit(solution)/shard_map/all_gather | solution.py:125
  210.7 38.0 %all-gather.1 = f32[32,4,2]{1,2,0:T(2,128)S(1)} all-gather(f32[1,4,2]{1,2,0:T(2,128)S(1)} %bitcast.294), channel_id=1, replica_groups=mesh['fsdp'=32,'sp'=16] {'fsdp'}, dimensions={0}, use_global_device_ids=true | all-gather | bytes 1056 | tf_op jit(solution)/shard_map/all_gather | solution.py:126
  258.5 13.7 %gather_fusion.5 = bf16[2048,2,128]{2,1,0:T(2,128)(2,1)} fusion(bf16[2048,2,128]{2,1,0:T(2,128)(2,1)S(1)} %reshape.298, s32[2048]{0:T(1024)S(1)} %fusion.46), kind=kCustom, calls=%fused_computation.5 | custom fusion | bytes 2105344 | tf_op jit(solution)/shard_map/gather | solution.py:120
  272.2 13.7 %gather_fusion.6 = bf16[2048,2,128]{2,1,0:T(2,128)(2,1)} fusion(bf16[2048,2,128]{2,1,0:T(2,128)(2,1)S(1)} %reshape.299, s32[2048]{0:T(1024)S(1)} %fusion.46), kind=kCustom, calls=%fused_computation.6 | custom fusion | bytes 2105344 | tf_op jit(solution)/shard_map/gather | solution.py:120
  285.9 11.8 %all-to-all-start.3 = ((bf16[128,16,256]{0,2,1:T(8,128)(2,1)}), bf16[128,16,256]{0,2,1:T(8,128)(2,1)}, u32[]{:S(2)}, u32[]{:S(2)}) async-start(bf16[128,16,256]{0,2,1:T(8,128)(2,1)} %bitcast.50), calls=%async_computation.3 | async-start | bytes 2097152 | tf_op jit(solution)/shard_map/all_to_all | solution.py:132
  298.5 7.0 %gather_fusion.4 = bf16[2048,2,128]{2,1,0:T(2,128)(2,1)S(1)} fusion(bf16[2048,2,128]{2,1,0:T(2,128)(2,1)S(1)} %reshape.297, s32[2048]{0:T(1024)S(1)} %fusion.46), kind=kCustom, calls=%fused_computation.4 | custom fusion | bytes 2105344 | tf_op jit(solution)/shard_map/gather | solution.py:120
  308.6 53.5 %while.62 = (s32[]{:T(128)}, f32[2,16,128,128]{3,2,1,0:T(8,128)}, f32[2,16,128,128]{3,2,1,0:T(8,128)}, bf16[2,16,128,128]{3,2,1,0:T(8,128)(2,1)}, bf16[2,16,128,...) while((s32[]{:T(128)}, f32[2,16,128,128]{3,2,1,0:T(8,128)}, ...), condition=%wide.region_7.8_spmd, body=%wide.region_0.7_spmd.sunk | while | flops 210636864 | bytes 52459220 | solution.py:138
  312.1 18.1 %while.65 = (s32[]{:T(128)}, f32[4,4,128,1]{2,1,3,0:T(4,128)S(1)}, f32[4,4,128,1]{2,1,3,0:T(4,128)S(1)}, f32[4,4,128,128]{3,2,1,0:T(8,128)}, bf16[4,4,128,128]{3...) while((s32[]{:T(128)}, f32[4,4,128,1]{2,1,3,0:T(4,128)S(1)}, ...), condition=%wide.region_6.6_spmd, body=%wide.region_3.5_spmd.sunk | while | flops 204079168 | bytes 9854725 | solution.py:58
  330.2 3.2 fusion.85
  338.9 18.1 %while.65 = (s32[]{:T(128)}, f32[4,4,128,1]{2,1,3,0:T(4,128)S(1)}, f32[4,4,128,1]{2,1,3,0:T(4,128)S(1)}, f32[4,4,128,128]{3,2,1,0:T(8,128)}, bf16[4,4,128,128]{3...) while((s32[]{:T(128)}, f32[4,4,128,1]{2,1,3,0:T(4,128)S(1)}, ...), condition=%wide.region_6.6_spmd, body=%wide.region_3.5_spmd.sunk | while | flops 204079168 | bytes 9854725 | solution.py:58
  357.0 3.2 fusion.85
  363.9 7.0 %gather_fusion.7 = bf16[2048,2,128]{2,1,0:T(2,128)(2,1)S(1)} fusion(bf16[2048,2,128]{2,1,0:T(2,128)(2,1)S(1)} %reshape.300, s32[2048]{0:T(1024)S(1)} %fusion.46), kind=kCustom, calls=%fused_computation.7 | custom fusion | bytes 2105344 | tf_op jit(solution)/shard_map/gather | solution.py:120
  371.2 131.0 %while.64 = (s32[]{:T(128)}, f32[2,128]{1,0:T(2,128)S(1)}, f32[2,128]{1,0:T(2,128)S(1)}, bf16[2,16,128,128]{3,2,1,0:T(8,128)(2,1)}, s32[16,6]{1,0:T(8,128)S(1)},...) while((s32[]{:T(128)}, f32[2,128]{1,0:T(2,128)S(1)}, ...), condition=%wide.region_14.15_spmd, body=%wide.region_8.14_spmd.sunk | while | flops 483327168 | bytes 43717104 | solution.py:146
  371.3 3.3 multiply_reduce_fusion.7
  378.8 52.8 %while.66 = (s32[]{:T(128)}, f32[16,128,128]{2,0,1:T(8,128)}, f32[4,4,128,128]{3,2,1,0:T(8,128)}, s32[4,4,6]{2,1,0:T(4,128)S(1)}, bf16[4,4,128,128]{3,2,1,0:T(8,...) while((s32[]{:T(128)}, f32[16,128,128]{2,0,1:T(8,128)}, ...), condition=%wide.region_11.11_spmd.clone, body=%wide.region_10.10_spmd.clone.sunk | while | flops 481494464 | bytes 21128336 | solution.py:103
  380.9 2.6 gather_fusion.1
  386.7 3.3 fusion.100
  399.0 4.6 fusion.100
  412.5 4.6 fusion.100
  426.0 4.6 fusion.100
  436.8 3.3 multiply_reduce_fusion.7
  444.3 52.8 %while.66 = (s32[]{:T(128)}, f32[16,128,128]{2,0,1:T(8,128)}, f32[4,4,128,128]{3,2,1,0:T(8,128)}, s32[4,4,6]{2,1,0:T(4,128)S(1)}, bf16[4,4,128,128]{3,2,1,0:T(8,...) while((s32[]{:T(128)}, f32[16,128,128]{2,0,1:T(8,128)}, ...), condition=%wide.region_11.11_spmd.clone, body=%wide.region_10.10_spmd.clone.sunk | while | flops 481494464 | bytes 21128336 | solution.py:103
  452.2 3.3 fusion.100
  464.5 4.6 fusion.100
  478.0 4.6 fusion.100
  491.5 4.6 fusion.100
  502.2 67.2 %all-reduce.2 = (f32[2,128]{1,0:T(2,128)S(1)}, f32[2,128]{1,0:T(2,128)S(1)}) all-reduce(f32[2,128]{1,0:T(2,128)S(1)} %get-tuple-element.262, f32[2,128]{1,0:T(2,128)S(1)} %get-tuple-element.263), channel_id=2, replica_groups=mesh['fsdp'=32,'sp'=16] {'fsdp'}, use_global_device_ids=true, to_apply=%region_15.16.clone | all-reduce | flops 512 | bytes 4096
  (338 shorter events, 155.2 us)
Async XLA Ops:
  2.9 18.5 %copy-start.13 = (bf16[1,128,4096]{2,1,0:T(8,128)(2,1)S(1)}, bf16[1,128,4096]{2,1,0:T(8,128)(2,1)}, u32[]{:S(2)}) copy-start(bf16[1,128,4096]{2,1,0:T(8,128)(2,1)} %param.18) | copy-start | bytes 3145732
  2.9 67.9 %all-to-all-start.1 = ((bf16[128,16,256]{0,2,1:T(8,128)(2,1)}), bf16[128,16,256]{0,2,1:T(8,128)(2,1)S(1)}, u32[]{:S(2)}, u32[]{:S(2)}) async-start(bf16[128,16,256]{0,2,1:T(8,128)(2,1)} %bitcast.34), calls=%async_computation.1 | async-start | bytes 2097152 | tf_op jit(solution)/shard_map/all_to_all | solution.py:130
  22.8 57.6 %copy-start.14 = (bf16[1,128,4096]{2,1,0:T(8,128)(2,1)S(1)}, bf16[1,128,4096]{2,1,0:T(8,128)(2,1)}, u32[]{:S(2)}) copy-start(bf16[1,128,4096]{2,1,0:T(8,128)(2,1)} %param.16) | copy-start | bytes 3145732
  70.9 39.6 %all-to-all-start.2 = ((bf16[128,16,256]{0,2,1:T(8,128)(2,1)}), bf16[128,16,256]{0,2,1:T(8,128)(2,1)S(1)}, u32[]{:S(2)}, u32[]{:S(2)}) async-start(bf16[128,16,256]{0,2,1:T(8,128)(2,1)} %bitcast.45), calls=%async_computation.2 | async-start | bytes 2097152 | tf_op jit(solution)/shard_map/all_to_all | solution.py:131
  81.7 33.0 %copy-start.16 = (s32[16,6]{0,1:T(8,128)S(1)}, s32[16,6]{0,1:T(8,128)}, u32[]{:S(2)}) copy-start(s32[16,6]{0,1:T(8,128)} %param.22) | copy-start | bytes 1156
  81.7 33.1 %copy-start.17 = (f32[2,4]{1,0:T(2,128)S(1)}, f32[2,4]{1,0:T(2,128)}, u32[]{:S(2)}) copy-start(f32[2,4]{1,0:T(2,128)} %param.20) | copy-start | bytes 100
  81.7 129.1 %copy-start.18 = (f32[2,4]{1,0:T(2,128)S(1)}, f32[2,4]{1,0:T(2,128)}, u32[]{:S(2)}) copy-start(f32[2,4]{1,0:T(2,128)} %param.21) | copy-start | bytes 100
  110.5 175.4 %all-to-all-start = ((bf16[128,16,256]{0,2,1:T(8,128)(2,1)}), bf16[128,16,256]{0,2,1:T(8,128)(2,1)S(1)}, u32[]{:S(2)}, u32[]{:S(2)}) async-start(bf16[128,16,256]{0,2,1:T(8,128)(2,1)} %bitcast.29), calls=%async_computation | async-start | bytes 2097152 | tf_op jit(solution)/shard_map/all_to_all | solution.py:129
  114.6 138.5 %copy-start.15 = (s32[2048]{0:T(1024)S(1)}, s32[2048]{0:T(1024)}, u32[]{:S(2)}) copy-start(s32[2048]{0:T(1024)} %param.23) | copy-start | bytes 24580
  285.9 76.3 %all-to-all-start.3 = ((bf16[128,16,256]{0,2,1:T(8,128)(2,1)}), bf16[128,16,256]{0,2,1:T(8,128)(2,1)}, u32[]{:S(2)}, u32[]{:S(2)}) async-start(bf16[128,16,256]{0,2,1:T(8,128)(2,1)} %bitcast.50), calls=%async_computation.3 | async-start | bytes 2097152 | tf_op jit(solution)/shard_map/all_to_all | solution.py:132
  305.6 1.2 copy-start.11
  305.6 1.5 copy-start.12
  308.6 2.7 copy-start.4
  308.6 3.5 copy-start.2
  310.2 1.9 copy-start.6
  330.2 3.3 copy-start.3
  330.2 3.3 copy-start.9
  330.2 3.8 copy-start.5
  334.0 1.4 copy-start.10
  335.4 2.7 copy-start.4
  335.4 3.5 copy-start.2
  336.9 1.9 copy-start.6
  357.0 3.3 copy-start.3
  357.0 3.3 copy-start.9
  357.0 3.8 copy-start.5
  360.7 1.4 copy-start.10
  371.2 3.3 copy-start.7
  403.6 1.1 copy-start.1
  435.1 1.6 copy-start.8
  436.8 3.3 copy-start.7
  469.1 1.1 copy-start.1
  500.6 1.6 copy-start.8
  (14 other events, 12.9 us)
where the time goes:
time: 574 us; the launch traced here: 571 us
  blocking collectives  201 us (35%)
  local copies, waits for them, and re-layouts  113 us (20%)
  matrix products  98.3 us (17%)
  waiting for transfers between devices  76.9 us (13%)
  starting transfers between devices  43.9 us (8%)
  other arithmetic  34.7 us (6%)
    all_gather x1, blocking collectives, shards(): lax.all_gather(gain_q, 'fsdp', axis=1, tiled=True)  95.8 us
    unnamed x1, blocking collectives  67.2 us
    all_to_all x1, waiting for transfers between devices, shards(): lax.all_to_all(split(key), 'sp', split_axis=1, concat_axis=0, tiled=True)  48.1 us
    gather x4, local copies, waits for them, and re-layouts, arrange(): rows = rows.reshape(-1, head_count, width)[order]  41.5 us
    all_gather x1, blocking collectives, shards(): lax.all_gather(gain_k, 'fsdp', axis=1, tiled=True)  38 us
    gather x32, local copies, waits for them, and re-layouts, window_rows(): taken = rows[picks]  37.6 us
    dot_general x8, matrix products, one_block(): jnp.einsum('tns,tnrd->srd', onehot, dkeys, precision=lax.Precision.HIGHEST)  34 us
    all_to_all x1, waiting for transfers between devices, shards(): lax.all_to_all(split(value), 'sp', split_axis=1, concat_axis=0, tiled=True)  28.8 us
  transfers between devices with their start and end apart: 4, of which 2 were waited for; matrix products, arithmetic and copies ran while one was open for 18% of the time, Pallas kernels for 0%

commit v1 on v0

v1 whole, which is shorter than its diff:
```python
import functools

import jax
import jax.numpy as jnp
from jax import lax
from jax.experimental import pallas as pl
from jax.experimental.pallas import tpu as pltpu
from jax.sharding import PartitionSpec as P

TILE = 128


def pack_kernel(head, heads, width, refs_in, out_ref, sems):
    copies = []
    for dest in range(out_ref.shape[0]):
        lanes = pl.ds((dest * heads + head) * width, width)
        for part, ref in enumerate(refs_in):
            copies.append(
                pltpu.make_async_copy(
                    ref.at[0, :, lanes],
                    out_ref.at[dest, :, pl.ds(part * width, width)],
                    sems.at[dest, part],
                )
            )
    for copy in copies:
        copy.start()
    for copy in copies:
        copy.wait()


def pack(arrays, head, heads, groups, width):
    tokens = arrays[0].shape[1]
    count = len(arrays)

    def body(*refs):
        pack_kernel(head, heads, width, refs[:count], refs[count], refs[count + 1])

    return pl.pallas_call(
        body,
        out_shape=jax.ShapeDtypeStruct((groups, tokens, count * width), jnp.bfloat16),
        in_specs=[pl.BlockSpec(memory_space=pl.ANY)] * count,
        out_specs=pl.BlockSpec(memory_space=pl.ANY),
        scratch_shapes=[pltpu.SemaphoreType.DMA((groups, count))],
        cost_estimate=pl.CostEstimate(
            flops=0, bytes_accessed=4 * groups * tokens * count * width, transcendentals=0
        ),
        name="pack_head",
    )(*arrays)


def head_kernel(
    head,
    win_ref,
    rows_ref,
    order_ref,
    gain_q_ref,
    gain_k_ref,
    out_ref,
    kv_ref,
    knt_ref,
    khat_ref,
    qhat_ref,
    qn_ref,
    qd_ref,
    accq_ref,
    acck_ref,
):
    tiles, count = win_ref.shape
    width = qn_ref.shape[-1]
    tokens = tiles * TILE
    scale = width ** (-0.5)
    gain_q = gain_q_ref[head : head + 1, :]
    gain_k = gain_k_ref[head : head + 1, :]
    qd_ref[...] = jnp.zeros_like(qd_ref)
    accq_ref[...] = jnp.zeros_like(accq_ref)
    acck_ref[...] = jnp.zeros_like(acck_ref)

    def unit_rows(rows):
        return rows * lax.rsqrt(jnp.mean(rows * rows, axis=-1, keepdims=True) + 1e-06)

    def arrange(step, carry):
        start = pl.multiple_of(step * 2 * TILE, 2 * TILE)
        places = order_ref[pl.ds(start, 2 * TILE), :]
        iota = lax.broadcasted_iota(jnp.int32, (2 * TILE, tokens), 1)
        onehot = jnp.where(places == iota, 1.0, 0.0).astype(jnp.bfloat16)
        picked = jnp.dot(onehot, rows_ref[...], preferred_element_type=jnp.float32)
        for half in range(2):
            tile = step * 2 + half
            part = picked[half * TILE : (half + 1) * TILE]
            qhat = unit_rows(part[:, :width])
            khat = unit_rows(part[:, width : 2 * width])
            qn = (qhat * gain_q).astype(jnp.bfloat16)
            kn = khat * gain_k
            kn16 = kn.astype(jnp.bfloat16)
            kv_ref[tile, :, :width] = kn16
            kv_ref[tile, :, width:] = part[:, 2 * width : 3 * width].astype(jnp.bfloat16)
            knt_ref[tile] = kn16.astype(jnp.float32).T.astype(jnp.bfloat16)
            khat_ref[tile] = khat
            qhat_ref[tile] = qhat.T
            qn_ref[tile] = qn
            qd_ref[tile, :TILE, :width] = qn
            qd_ref[tile, TILE:, width:] = part[:, 3 * width :].astype(jnp.bfloat16)
        return carry

    lax.fori_loop(0, tiles // 2, arrange, 0)

    def attend(tile, carry):
        picks = [win_ref[tile, n] for n in range(count)]
        keys_values = jnp.concatenate([kv_ref[pick] for pick in picks], axis=0)
        both = lax.dot_general(
            keys_values, qd_ref[tile], (((1,), (1,)), ((), ())), preferred_element_type=jnp.float32
        )
        scores, dprobs = both[:, :TILE], both[:, TILE:]
        top = jnp.max(scores, axis=0, keepdims=True)
        weights = jnp.exp((scores - top) * scale)
        inverse = 1.0 / jnp.sum(weights, axis=0, keepdims=True)
        probs = weights * inverse
        rounded = probs.astype(jnp.bfloat16).astype(jnp.float32)
        rowterm = jnp.sum(rounded * dprobs, axis=0, keepdims=True)
        dscores = (probs * (dprobs - rowterm)).astype(jnp.bfloat16)
        keys_t = jnp.concatenate([knt_ref[pick] for pick in picks], axis=1)
        dquery_t = jnp.dot(keys_t, dscores, preferred_element_type=jnp.float32)
        accq_ref[...] += dquery_t * qhat_ref[tile]
        dkeys = jnp.dot(dscores, qn_ref[tile], preferred_element_type=jnp.float32)
        total = dkeys[:TILE] * khat_ref[picks[0]]
        for n in range(1, count):
            total = total + dkeys[n * TILE : (n + 1) * TILE] * khat_ref[picks[n]]
        acck_ref[...] += total
        return carry

    lax.fori_loop(0, tiles, attend, 0)
    out_ref[0:1, :] = jnp.sum(accq_ref[...].T, axis=0, keepdims=True) * scale
    out_ref[1:2, :] = jnp.sum(acck_ref[...], axis=0, keepdims=True) * scale


def head_terms(rows, order_column, gain_q, gain_k, windows, head):
    tokens = rows.shape[0]
    tiles, count = windows.shape
    width = gain_q.shape[-1]
    vmem = pl.BlockSpec(memory_space=pltpu.VMEM)
    return pl.pallas_call(
        functools.partial(head_kernel, head),
        out_shape=jax.ShapeDtypeStruct((2, width), jnp.float32),
        in_specs=[pl.BlockSpec(memory_space=pltpu.SMEM), vmem, vmem, vmem, vmem],
        out_specs=vmem,
        scratch_shapes=[
            pltpu.VMEM((tiles, TILE, 2 * width), jnp.bfloat16),
            pltpu.VMEM((tiles, width, TILE), jnp.bfloat16),
            pltpu.VMEM((tiles, TILE, width), jnp.float32),
            pltpu.VMEM((tiles, width, TILE), jnp.float32),
            pltpu.VMEM((tiles, TILE, width), jnp.bfloat16),
            pltpu.VMEM((tiles, 2 * TILE, 2 * width), jnp.bfloat16),
            pltpu.VMEM((width, TILE), jnp.float32),
            pltpu.VMEM((TILE, width), jnp.float32),
        ],
        compiler_params=pltpu.CompilerParams(vmem_limit_bytes=40 * 2**20),
        cost_estimate=pl.CostEstimate(
            flops=2 * tokens * tokens * 4 * width + 10 * tokens * count * TILE * width,
            bytes_accessed=rows.size * 2,
            transcendentals=tokens * count * TILE,
        ),
        name="head_terms",
    )(windows, rows, order_column, gain_q, gain_k)


def shards(query, key, value, cotangent, gain_q, gain_k, windows, order):
    groups = lax.axis_size("sp")
    spread = lax.axis_size("fsdp")
    tokens = query.shape[1]
    flat = query.shape[2]
    heads = gain_q.shape[0]
    width = flat // (groups * heads)
    own = gain_q.shape[1]
    arrays = (query, key, value, cotangent)

    def exchange(packed):
        rows = lax.all_to_all(packed, "sp", split_axis=0, concat_axis=0, tiled=True)
        return rows.reshape(groups * tokens, len(arrays) * width)

    packed = [pack(arrays, head, heads, groups, width) for head in range(heads)]
    gains = lax.all_gather(jnp.stack([gain_q, gain_k]), "fsdp", axis=2, tiled=True)
    order_column = order.reshape(order.shape[0], 1)
    terms = []
    for head in range(heads):
        rows = exchange(packed[head])
        terms.append(head_terms(rows, order_column, gains[0], gains[1], windows, head))
    stacked = jnp.stack(terms).reshape(heads, 2, spread, own)
    stacked = jnp.transpose(stacked, (2, 1, 0, 3)).reshape(spread, 2 * heads * own)
    arrived = lax.all_to_all(stacked, "fsdp", split_axis=0, concat_axis=0, tiled=True)
    sums = jnp.sum(arrived, axis=0).reshape(2, heads, own)
    return (sums[0], sums[1])


def solution(mesh):
    placed = (
        P("fsdp", "sp", None),
        P("fsdp", "sp", None),
        P("fsdp", "sp", None),
        P("fsdp", "sp", None),
        P("sp", "fsdp"),
        P("sp", "fsdp"),
        P(),
        P(),
    )
    return jax.shard_map(
        shards,
        mesh=mesh,
        in_specs=placed,
        out_specs=(P("sp", "fsdp"), P("sp", "fsdp")),
        check_vma=False,
    )
```

time: 574 us -> 379 us (0.66)
  Pallas kernels: 0 us -> 180 us
  local copies, waits for them, and re-layouts: 113 us -> 2.66 us
  matrix products: 98.3 us -> 0 us
  blocking collectives: 201 us -> 134 us
  waiting for transfers between devices: 76.9 us -> 31.5 us
  other arithmetic: 34.7 us -> 0.06 us
  starting transfers between devices: 43.9 us -> 27.2 us
    pallas_call x0 -> x4, Pallas kernels: none -> 180 us  [the longest x2 130 us: pack(): pl.pallas_call(body, out_shape=jax.ShapeDtypeStruct((groups, tokens, coun...]
    dot_general x56 -> x0, matrix products: 98.3 us -> none  [the longest x8 34 us: one_block(): jnp.einsum('tns,tnrd->srd', onehot, dkeys, precision=lax.Precision.HIGHEST)]
    gather x36 -> x0, local copies, waits for them, and re-layouts: 79.1 us -> none  [the longest x4 41.5 us: arrange(): rows = rows.reshape(-1, head_count, width)[order]]
    unnamed x1 -> x0, blocking collectives: 67.2 us -> none
    all_to_all x4 -> x2, waiting for transfers between devices: 76.9 us -> 31.5 us  [exchange(): rows = lax.all_to_all(packed, 'sp', split_axis=0, concat_axis=0, tiled=True)]
    reduce_sum x18 -> x1, other arithmetic: 18.9 us -> 0.05 us  [shards(): sums = jnp.sum(arrived, axis=0).reshape(2, heads, own)]
    all_to_all x4 -> x2, starting transfers between devices: 43.9 us -> 27.2 us  [exchange(): rows = lax.all_to_all(packed, 'sp', split_axis=0, concat_axis=0, tiled=True)]
    all_to_all x0 -> x1, blocking collectives: none -> 11.4 us  [shards(): lax.all_to_all(stacked, 'fsdp', split_axis=0, concat_axis=0, tiled=True)]
  transfers between devices with their start and end apart: 4 -> 2, of which waited for: 2 -> 1; matrix products, arithmetic and copies ran while one was open for 18% -> 0% of each run, Pallas kernels for 0% -> 24%
where the time goes in v1:
time: 379 us; the launch traced here: 376 us
  Pallas kernels  180 us (47%)
  blocking collectives  134 us (35%)
  waiting for transfers between devices  31.5 us (8%)
  starting transfers between devices  27.2 us (7%)
    pallas_call x2, Pallas kernels, pack(): pl.pallas_call(body, out_shape=jax.ShapeDtypeStruct((groups, tokens, coun...  130 us
    all_gather x1, blocking collectives, shards(): lax.all_gather(jnp.stack([gain_q, gain_k]), 'fsdp', axis=2, tiled=True)  123 us
    pallas_call x2, Pallas kernels, head_terms(): pl.pallas_call(functools.partial(head_kernel, head), out_shape=jax.ShapeD...  49.2 us
    all_to_all x2, waiting for transfers between devices, exchange(): rows = lax.all_to_all(packed, 'sp', split_axis=0, concat_axis=0, tiled=True)  31.5 us
    all_to_all x2, starting transfers between devices, exchange(): rows = lax.all_to_all(packed, 'sp', split_axis=0, concat_axis=0, tiled=True)  27.2 us
    all_to_all x1, blocking collectives, shards(): lax.all_to_all(stacked, 'fsdp', split_axis=0, concat_axis=0, tiled=True)  11.4 us
  transfers between devices with their start and end apart: 2, of which 1 were waited for; matrix products, arithmetic and copies ran while one was open for 0% of the time, Pallas kernels for 24%

profile of v1, /device:TPU:1, one launch (start us, length us, event | category | flops | bytes accessed | tf_op | source)
XLA Modules:
  0.0 376.1 jit_solution(11768629886130327229)
XLA Ops:
  0.6 65.2 %pack_head.3 = bf16[16,128,512]{2,1,0:T(8,128)(2,1)} custom-call(bf16[1,128,4096]{2,1,0:T(8,128)(2,1)} %refs_0_.3, bf16[1,128,4096]{2,1,0:T(8,128)(2,1)} %refs_1_.3, bf16[1,128,4096]{2,1,0:T(8,128)(2,1)} %refs_2_.3, bf16[1,128,4096]{2,1,0:T(8,128)(2,1)} %refs_3_.3), custom_call_target="tpu_custom_call" | custom-call | bytes 4194304 | tf_op jit(solution)/shard_map/pack_head/pallas_call | solution.py:38
  65.8 18.4 %all-to-all-start.1 = ((bf16[16,128,512]{2,1,0:T(8,128)(2,1)}), bf16[16,128,512]{2,1,0:T(8,128)(2,1)S(1)}, u32[]{:S(2)}, u32[]{:S(2)}) async-start(bf16[16,128,512]{2,1,0:T(8,128)(2,1)} %pack_head.3), calls=%async_computation.1 | async-start | bytes 4194304 | tf_op jit(solution)/shard_map/all_to_all | solution.py:177
  84.2 65.2 %pack_head.2 = bf16[16,128,512]{2,1,0:T(8,128)(2,1)} custom-call(bf16[1,128,4096]{2,1,0:T(8,128)(2,1)} %refs_0_.3, bf16[1,128,4096]{2,1,0:T(8,128)(2,1)} %refs_1_.3, bf16[1,128,4096]{2,1,0:T(8,128)(2,1)} %refs_2_.3, bf16[1,128,4096]{2,1,0:T(8,128)(2,1)} %refs_3_.3), custom_call_target="tpu_custom_call" | custom-call | bytes 4194304 | tf_op jit(solution)/shard_map/pack_head/pallas_call | solution.py:38
  149.5 0.0 copy-start.2
  149.5 0.0 copy-start.3
  149.5 0.0 copy-start.1
  149.5 0.0 copy-start
  149.5 31.5 %all-to-all-done.1 = bf16[16,128,512]{2,1,0:T(8,128)(2,1)S(1)} async-done(((bf16[16,128,512]{2,1,0:T(8,128)(2,1)}), bf16[16,128,512]{2,1,0:T(8,128)(2,1)S(1)}, u32[]{:S(2)}, u32[]{:S(2)}) %all-to-all-start.1) | async-done | bytes 2097184 | tf_op jit(solution)/shard_map/all_to_all | solution.py:177
  181.0 8.8 %all-to-all-start = ((bf16[16,128,512]{2,1,0:T(8,128)(2,1)}), bf16[16,128,512]{2,1,0:T(8,128)(2,1)}, u32[]{:S(2)}, u32[]{:S(2)}) async-start(bf16[16,128,512]{2,1,0:T(8,128)(2,1)} %pack_head.2), calls=%async_computation | async-start | bytes 4194304 | tf_op jit(solution)/shard_map/all_to_all | solution.py:177
  189.8 0.0 copy-done.2
  189.8 0.0 copy-done.3
  189.9 0.1 copy.17
  190.0 0.0 copy-done.1
  190.0 0.1 copy.20.win_ref
  190.0 122.9 %all_gather.3 = f32[2,2,128]{1,0,2:T(2,128)S(1)} all-gather(f32[2,2,4]{1,0,2:T(2,128)S(1)} %copy.17), channel_id=1, replica_groups=mesh['fsdp'=32,'sp'=16] {'fsdp'}, dimensions={2}, use_global_device_ids=true | all-gather | bytes 2112 | tf_op jit(solution)/shard_map/all_gather | solution.py:181
  312.9 0.1 fusion
  313.0 0.1 copy.29
  313.1 0.1 copy.28
  313.2 0.4 copy.21.order_ref
  313.6 24.2 %head_terms.3 = f32[2,128]{1,0:T(2,128)S(1)} custom-call(s32[16,6]{1,0:T(8,128)S(1)} %copy.20.win_ref, bf16[2048,512]{1,0:T(8,128)(2,1)S(1)} %bitcast.10, s32[2048,1]{1,0:T(8,128)S(1)} %copy.21.order_ref, f32[2,128]{1,0:T(2,128)S(1)} %bitcast.13, f32[2,128]{1,0:T(2,128)S(1)} %bitcast.11), custom_call_target="tpu_custom_call" | custom-call | flops 6308233216 | bytes 2097152 | tf_op jit(solution)/shard_map/head_terms/pallas_call | solution.py:141
  337.7 0.1 stack.22
  337.8 0.1 copy.25
  337.9 0.0 all-to-all-done
  337.9 25.1 %head_terms.2 = f32[2,128]{1,0:T(2,128)S(1)} custom-call(s32[16,6]{1,0:T(8,128)S(1)} %copy.20.win_ref, bf16[2048,512]{1,0:T(8,128)(2,1)} %bitcast.rows_ref, s32[2048,1]{1,0:T(8,128)S(1)} %copy.21.order_ref, f32[2,128]{1,0:T(2,128)S(1)} %bitcast.14, f32[2,128]{1,0:T(2,128)S(1)} %bitcast.12), custom_call_target="tpu_custom_call" | custom-call | flops 6308233216 | bytes 2097152 | tf_op jit(solution)/shard_map/head_terms/pallas_call | solution.py:141
  363.0 0.1 stack.21
  363.1 0.1 copy.24
  363.2 0.1 copy.27
  363.3 11.4 %all_to_all.19 = f32[32,1,16]{2,1,0:T(1,128)S(1)} all-to-all(f32[32,1,16]{2,1,0:T(1,128)S(1)} %copy.27), channel_id=1, replica_groups=mesh['fsdp'=32,'sp'=16] {'fsdp'}, dimensions={0} | all-to-all | bytes 4096 | tf_op jit(solution)/shard_map/all_to_all | solution.py:189
  374.7 0.1 reduce_sum.9
  374.8 0.1 fusion.1
  374.8 0.6 squeeze.17
  375.5 0.6 squeeze.16
  (4 shorter events, 0.0 us)
Async XLA Ops:
  65.8 115.2 %all-to-all-start.1 = ((bf16[16,128,512]{2,1,0:T(8,128)(2,1)}), bf16[16,128,512]{2,1,0:T(8,128)(2,1)S(1)}, u32[]{:S(2)}, u32[]{:S(2)}) async-start(bf16[16,128,512]{2,1,0:T(8,128)(2,1)} %pack_head.3), calls=%async_computation.1 | async-start | bytes 4194304 | tf_op jit(solution)/shard_map/all_to_all | solution.py:177
  149.5 40.4 %copy-start.2 = (f32[2,4]{1,0:T(2,128)S(1)}, f32[2,4]{1,0:T(2,128)}, u32[]{:S(2)}) copy-start(f32[2,4]{1,0:T(2,128)} %param.13) | copy-start | bytes 100
  149.5 40.4 %copy-start.3 = (f32[2,4]{1,0:T(2,128)S(1)}, f32[2,4]{1,0:T(2,128)}, u32[]{:S(2)}) copy-start(f32[2,4]{1,0:T(2,128)} %param.12) | copy-start | bytes 100
  149.5 40.5 %copy-start.1 = (s32[16,6]{0,1:T(8,128)S(1)}, s32[16,6]{0,1:T(8,128)}, u32[]{:S(2)}) copy-start(s32[16,6]{0,1:T(8,128)} %param.14) | copy-start | bytes 1156
  149.5 163.7 %copy-start = (s32[2048]{0:T(1024)S(1)}, s32[2048]{0:T(1024)}, u32[]{:S(2)}) copy-start(s32[2048]{0:T(1024)} %param.15) | copy-start | bytes 24580
  181.0 156.9 %all-to-all-start = ((bf16[16,128,512]{2,1,0:T(8,128)(2,1)}), bf16[16,128,512]{2,1,0:T(8,128)(2,1)}, u32[]{:S(2)}, u32[]{:S(2)}) async-start(bf16[16,128,512]{2,1,0:T(8,128)(2,1)} %pack_head.2), calls=%async_computation | async-start | bytes 4194304 | tf_op jit(solution)/shard_map/all_to_all | solution.py:177

commit v2 on v1

v2 whole, which is shorter than its diff:
```python
import jax
import jax.numpy as jnp
from jax import lax
from jax.experimental import pallas as pl
from jax.experimental.pallas import tpu as pltpu
from jax.sharding import PartitionSpec as P

TILE = 128
LOG2E = 1.4426950408889634
PARTS = 4


def pack(arrays, groups, heads, width):
    tokens, flat = arrays[0].shape[1:]
    rows = heads * PARTS
    chunks = 4
    span = flat // chunks

    def body(*refs):
        ins, out_ref = refs[:PARTS], refs[PARTS]
        held_ref, ready_ref, wide_ref, in_sems, out_sems = refs[PARTS + 1 :]
        arrivals = []
        for chunk in range(chunks):
            lanes = slice(chunk * span, (chunk + 1) * span)
            arrivals.append(
                [
                    pltpu.make_async_copy(
                        ins[part].at[0, :, lanes],
                        held_ref.at[part, :, lanes],
                        in_sems.at[chunk, part],
                    )
                    for part in range(PARTS)
                ]
            )
            for copy in arrivals[-1]:
                copy.start()
        leaving = []
        for dest in range(groups):
            if dest % (groups // chunks) == 0:
                for copy in arrivals[dest // (groups // chunks)]:
                    copy.wait()
            for head in range(heads):
                for part in range(PARTS):
                    start = (dest * heads + head) * width
                    block = held_ref[part, :, start : start + width].astype(jnp.float32)
                    wide_ref[dest % 2, pl.ds(head * PARTS + part, tokens, stride=rows), :] = block
            ready_ref[dest] = (
                wide_ref[dest % 2].reshape(tokens, rows, width).astype(jnp.bfloat16)
            )
            leaving.append(
                pltpu.make_async_copy(ready_ref.at[dest], out_ref.at[dest], out_sems.at[dest])
            )
            leaving[-1].start()
        for copy in leaving:
            copy.wait()

    return pl.pallas_call(
        body,
        out_shape=jax.ShapeDtypeStruct((groups, tokens, rows, width), jnp.bfloat16),
        in_specs=[pl.BlockSpec(memory_space=pl.ANY)] * PARTS,
        out_specs=pl.BlockSpec(memory_space=pl.ANY),
        scratch_shapes=[
            pltpu.VMEM((PARTS, tokens, flat), jnp.bfloat16),
            pltpu.VMEM((groups, tokens, rows, width), jnp.bfloat16),
            pltpu.VMEM((2, tokens * rows, width), jnp.float32),
            pltpu.SemaphoreType.DMA((chunks, PARTS)),
            pltpu.SemaphoreType.DMA((groups,)),
        ],
        compiler_params=pltpu.CompilerParams(vmem_limit_bytes=56 * 2**20),
        cost_estimate=pl.CostEstimate(
            flops=0, bytes_accessed=4 * groups * tokens * rows * width, transcendentals=0
        ),
        name="pack_tokens",
    )(*arrays)


def terms_kernel(
    win_ref,
    order_ref,
    rows_ref,
    gain_q_ref,
    gain_k_ref,
    out_ref,
    wide_ref,
    kv_ref,
    khat_ref,
    qd_ref,
    qe_ref,
    acc_ref,
    *stages,
):
    tiles, count = win_ref.shape
    tokens = tiles * TILE
    heads, width = gain_q_ref.shape
    rows = heads * PARTS
    scale = width ** (-0.5)
    both_refs, ds_refs = stages[:heads], stages[heads:]
    acc_ref[...] = jnp.zeros_like(acc_ref)

    def gather(step, carry):
        for n in range(16):
            place = step * 16 + n
            token = rows_ref[order_ref[place]].astype(jnp.float32)
            wide_ref[pl.ds(pl.multiple_of(place * rows, rows), rows), :] = token
        return carry

    lax.fori_loop(0, tokens // 16, gather, 0)

    def unit_rows(block):
        return block * lax.rsqrt(jnp.mean(block * block, axis=-1, keepdims=True) + 1e-06)

    def arrange(tile, carry):
        for head in range(heads):

            def take(part):
                return wide_ref[
                    pl.ds(tile * TILE * rows + head * PARTS + part, TILE, stride=rows), :
                ]

            qfull = unit_rows(take(0)) * gain_q_ref[head : head + 1, :]
            khat = unit_rows(take(1))
            qn = qfull.astype(jnp.bfloat16)
            kv_ref[head, tile, :, :width] = (khat * gain_k_ref[head : head + 1, :]).astype(
                jnp.bfloat16
            )
            kv_ref[head, tile, :, width:] = take(2).astype(jnp.bfloat16)
            khat_ref[head, tile] = khat
            qd_ref[head, tile, :, :width] = qn
            qd_ref[head, tile, :, width:] = take(3).astype(jnp.bfloat16)
            qe_ref[head, tile] = (qfull - qn.astype(jnp.float32)).astype(jnp.bfloat16)
        return carry

    lax.fori_loop(0, tiles, arrange, 0)
    blank = jnp.zeros((TILE, width), jnp.bfloat16)
    spans = [slice(n * TILE, (n + 1) * TILE) for n in range(count)]

    def fold(block):
        return jnp.sum(block.reshape(-1, 8, width), axis=0)

    def products(head, tile):
        qn, grad = qd_ref[head, tile, :, :width], qd_ref[head, tile, :, width:]
        both_refs[head][...] = lax.dot_general(
            jnp.concatenate([kv_ref[head, win_ref[tile, n]] for n in range(count)], axis=0),
            jnp.concatenate(
                [
                    jnp.concatenate([qn, blank], axis=1),
                    jnp.concatenate([blank, grad], axis=1),
                ],
                axis=0,
            ),
            (((1,), (1,)), ((), ())),
            preferred_element_type=jnp.float32,
        )

    def softmax_grad(head):
        both_ref, ds_ref = both_refs[head], ds_refs[head]
        tops, sums = [], []
        for span in spans:
            scores = both_ref[span, :TILE]
            top = jnp.max(scores, axis=0, keepdims=True)
            weights = jnp.exp2((scores - top) * (scale * LOG2E))
            both_ref[span, :TILE] = weights
            tops.append(top)
            sums.append(jnp.sum(weights, axis=0, keepdims=True))
        highest = tops[0]
        for top in tops[1:]:
            highest = jnp.maximum(highest, top)
        factors = [jnp.exp2((top - highest) * (scale * LOG2E)) for top in tops]
        total = sums[0] * factors[0]
        for n in range(1, count):
            total = total + sums[n] * factors[n]
        inverse = 1.0 / total
        factors = [factor * inverse for factor in factors]
        rowterm = jnp.zeros((8, TILE), jnp.float32)
        for span, factor in zip(spans, factors):
            rounded = (both_ref[span, :TILE] * factor).astype(jnp.bfloat16).astype(jnp.float32)
            rowterm = rowterm + fold(rounded * both_ref[span, TILE:])
        rowterm = jnp.sum(rowterm, axis=0, keepdims=True)
        for span, factor in zip(spans, factors):
            probs = both_ref[span, :TILE] * factor
            ds_ref[span, :] = (probs * (both_ref[span, TILE:] - rowterm)).astype(jnp.bfloat16)

    def key_terms(head, tile):
        sent = jnp.dot(
            ds_refs[head][...],
            jnp.concatenate([qd_ref[head, tile, :, :width], qe_ref[head, tile]], axis=1),
            preferred_element_type=jnp.float32,
        )
        sum_q, sum_k = acc_ref[0, head], acc_ref[1, head]
        for n, span in enumerate(spans):
            pick = win_ref[tile, n]
            dkey, rest = sent[span, :width], sent[span, width:]
            kn = kv_ref[head, pick, :, :width].astype(jnp.float32)
            sum_q = sum_q + fold(kn * (dkey + rest))
            sum_k = sum_k + fold(khat_ref[head, pick] * dkey)
        acc_ref[0, head] = sum_q
        acc_ref[1, head] = sum_k

    last = heads - 1
    for ds_ref in ds_refs:
        ds_ref[...] = jnp.zeros_like(ds_ref)
    products(0, 0)

    def attend(tile, carry):
        for head in range(heads):
            if head < last:
                products(head + 1, tile)
            else:
                products(0, jnp.minimum(tile + 1, tiles - 1))
            softmax_grad(head)
            if head > 0:
                key_terms(head - 1, tile)
            else:
                key_terms(last, jnp.maximum(tile - 1, 0))
        return carry

    lax.fori_loop(0, tiles, attend, 0)
    key_terms(last, tiles - 1)
    for head in range(heads):
        row = slice(head, head + 1)
        sums_q = jnp.sum(acc_ref[0, head], axis=0, keepdims=True)
        sums_k = jnp.sum(acc_ref[1, head], axis=0, keepdims=True)
        out_ref[0, row, :] = sums_q * scale / gain_q_ref[row, :]
        out_ref[1, row, :] = sums_k * scale


def head_terms(rows, order, gain_q, gain_k, windows):
    tokens = rows.shape[0]
    tiles, count = windows.shape
    heads, width = gain_q.shape
    vmem = pl.BlockSpec(memory_space=pltpu.VMEM)
    smem = pl.BlockSpec(memory_space=pltpu.SMEM)
    return pl.pallas_call(
        terms_kernel,
        out_shape=jax.ShapeDtypeStruct((2, heads, width), jnp.float32),
        in_specs=[smem, smem, vmem, vmem, vmem],
        out_specs=vmem,
        scratch_shapes=[
            pltpu.VMEM((tokens * heads * PARTS, width), jnp.float32),
            pltpu.VMEM((heads, tiles, TILE, 2 * width), jnp.bfloat16),
            pltpu.VMEM((heads, tiles, TILE, width), jnp.float32),
            pltpu.VMEM((heads, tiles, TILE, 2 * width), jnp.bfloat16),
            pltpu.VMEM((heads, tiles, TILE, width), jnp.bfloat16),
            pltpu.VMEM((2, heads, 8, width), jnp.float32),
            *[pltpu.VMEM((count * TILE, 2 * TILE), jnp.float32)] * heads,
            *[pltpu.VMEM((count * TILE, TILE), jnp.bfloat16)] * heads,
        ],
        compiler_params=pltpu.CompilerParams(vmem_limit_bytes=28 * 2**20),
        cost_estimate=pl.CostEstimate(
            flops=heads * 10 * tokens * count * TILE * width,
            bytes_accessed=rows.size * 2,
            transcendentals=heads * tokens * count * TILE,
        ),
        name="head_terms",
    )(windows, order, rows, gain_q, gain_k)


def shards(query, key, value, cotangent, gain_q, gain_k, windows, order):
    groups = lax.axis_size("sp")
    spread = lax.axis_size("fsdp")
    tokens = query.shape[1]
    heads, own = gain_q.shape
    width = own * spread

    shares = jnp.stack([gain_q, gain_k]).reshape(1, 2 * heads * own)
    shares = jnp.broadcast_to(shares, (spread, 2 * heads * own))
    shares = lax.all_to_all(shares, "fsdp", split_axis=0, concat_axis=0, tiled=True)
    gains = jnp.transpose(shares.reshape(spread, 2, heads, own), (1, 2, 0, 3))
    gains = gains.reshape(2, heads, width)

    packed = pack((query, key, value, cotangent), groups, heads, width)
    packed, gains = lax.optimization_barrier((packed, gains))
    rows = lax.all_to_all(packed, "sp", split_axis=0, concat_axis=0, tiled=True)
    rows = rows.reshape(groups * tokens, heads * PARTS, width)
    terms = head_terms(rows, order, gains[0], gains[1], windows)
    terms = jnp.transpose(terms.reshape(2, heads, spread, own), (2, 0, 1, 3))
    terms = terms.reshape(spread, 2 * heads * own)
    arrived = lax.all_to_all(terms, "fsdp", split_axis=0, concat_axis=0, tiled=True)
    sums = jnp.sum(arrived, axis=0).reshape(2, heads, own)
    return (sums[0], sums[1])


def solution(mesh):
    placed = (
        P("fsdp", "sp", None),
        P("fsdp", "sp", None),
        P("fsdp", "sp", None),
        P("fsdp", "sp", None),
        P("sp", "fsdp"),
        P("sp", "fsdp"),
        P(),
        P(),
    )
    return jax.shard_map(
        shards,
        mesh=mesh,
        in_specs=placed,
        out_specs=(P("sp", "fsdp"), P("sp", "fsdp")),
        check_vma=False,
    )
```

time: 379 us -> 266 us (0.70)
  waiting for transfers between devices: 31.5 us -> 188 us
  Pallas kernels: 180 us -> 26.6 us
  blocking collectives: 134 us -> 18.7 us
    all_to_all x2, waiting for transfers between devices: 31.5 us -> 188 us  [the longest x1 185 us: shards(): rows = lax.all_to_all(packed, 'sp', split_axis=0, concat_axis=0, tiled=True)]
    pallas_call x4 -> x2, Pallas kernels: 180 us -> 26.6 us  [the longest x1 21.9 us: head_terms(): pl.pallas_call(terms_kernel, out_shape=jax.ShapeDtypeStruct((2, heads, wi...]
    all_gather x1 -> x0, blocking collectives: 123 us -> none  [shards(): lax.all_gather(jnp.stack([gain_q, gain_k]), 'fsdp', axis=2, tiled=True)]
    all_to_all x1, blocking collectives: 11.4 us -> 18.7 us  [shards(): lax.all_to_all(terms, 'fsdp', split_axis=0, concat_axis=0, tiled=True)]
  transfers between devices with their start and end apart: 2 -> 2, of which waited for: 1 -> 2; matrix products, arithmetic and copies ran while one was open for 0% -> 0% of each run, Pallas kernels for 24% -> 2%
where the time goes in v2:
time: 266 us; the launch traced here: 262 us
  waiting for transfers between devices  188 us (71%)
  Pallas kernels  26.6 us (10%)
  starting transfers between devices  24.8 us (9%)
  blocking collectives  18.7 us (7%)
  local copies, waits for them, and re-layouts  2.71 us (1%)
    all_to_all x1, waiting for transfers between devices, shards(): rows = lax.all_to_all(packed, 'sp', split_axis=0, concat_axis=0, tiled=True)  185 us
    pallas_call x1, Pallas kernels, head_terms(): pl.pallas_call(terms_kernel, out_shape=jax.ShapeDtypeStruct((2, heads, wi...  21.9 us
    all_to_all x1, blocking collectives, shards(): lax.all_to_all(terms, 'fsdp', split_axis=0, concat_axis=0, tiled=True)  18.7 us
    all_to_all x1, starting transfers between devices, shards(): rows = lax.all_to_all(packed, 'sp', split_axis=0, concat_axis=0, tiled=True)  14.5 us
    all_to_all x1, starting transfers between devices, shards(): lax.all_to_all(shares, 'fsdp', split_axis=0, concat_axis=0, tiled=True)  10.3 us
  transfers between devices with their start and end apart: 2, of which 2 were waited for; matrix products, arithmetic and copies ran while one was open for 0% of the time, Pallas kernels for 2%

profile of v2, /device:TPU:1, one launch (start us, length us, event | category | flops | bytes accessed | tf_op | source)
XLA Modules:
  0.0 262.2 jit_solution(5824270243098425345)
XLA Ops:
  0.6 0.7 pad_maximum_fusion
  1.3 0.1 broadcast_in_dim.7
  1.4 0.6 broadcast_in_dim.8
  2.0 10.3 %all-to-all-start = ((f32[32,1,16]{2,1,0:T(1,128)}), f32[32,1,16]{2,1,0:T(1,128)S(1)}, u32[]{:S(2)}, u32[]{:S(2)}) async-start(f32[32,1,16]{2,1,0:T(1,128)} %broadcast_in_dim.8), calls=%async_computation | async-start | bytes 32768 | tf_op jit(solution)/shard_map/all_to_all | solution.py:267
  12.4 4.7 %pack_tokens.1 = bf16[16,128,8,128]{3,2,1,0:T(8,128)(2,1)} custom-call(bf16[1,128,4096]{2,1,0:T(8,128)(2,1)} %refs_0_.1, bf16[1,128,4096]{2,1,0:T(8,128)(2,1)} %refs_1_.1, bf16[1,128,4096]{2,1,0:T(8,128)(2,1)} %refs_2_.1, bf16[1,128,4096]{2,1,0:T(8,128)(2,1)} %refs_3_.1), custom_call_target="tpu_custom_call" | custom-call | bytes 8388608 | tf_op jit(solution)/shard_map/pack_tokens/pallas_call | solution.py:57
  17.1 2.6 all-to-all-done
  19.7 0.1 copy.14
  19.7 0.1 copy.15
  19.8 0.1 reshape.52
  20.0 0.0 copy-start.1
  20.0 0.0 copy-start
  20.0 14.5 %all-to-all-start.1 = ((bf16[16,128,8,128]{3,2,1,0:T(8,128)(2,1)}), bf16[16,128,8,128]{3,2,1,0:T(8,128)(2,1)}, u32[]{:S(2)}, u32[]{:S(2)}) async-start(bf16[16,128,8,128]{3,2,1,0:T(8,128)(2,1)} %pack_tokens.1), calls=%async_computation.1 | async-start | bytes 8388608 | tf_op jit(solution)/shard_map/all_to_all | solution.py:273
  34.5 0.0 copy-done.1
  34.5 0.1 copy.16.win_ref
  34.6 185.3 %all-to-all-done.1 = bf16[16,128,8,128]{3,2,1,0:T(8,128)(2,1)} async-done(((bf16[16,128,8,128]{3,2,1,0:T(8,128)(2,1)}), bf16[16,128,8,128]{3,2,1,0:T(8,128)(2,1)}, u32[]{:S(2)}, u32[]{:S(2)}) %all-to-all-start.1) | async-done | bytes 4194336 | tf_op jit(solution)/shard_map/all_to_all | solution.py:273
  219.9 0.0 copy-done
  219.9 21.9 %head_terms.1 = f32[2,2,128]{2,1,0:T(2,128)S(1)} custom-call(s32[16,6]{1,0:T(8,128)S(1)} %copy.16.win_ref, s32[2048]{0:T(1024)S(1)} %copy-done, bf16[2048,8,128]{2,1,0:T(8,128)(2,1)} %bitcast.4.rows_ref, f32[2,128]{1,0:T(2,128)S(1)} %get-tuple-element.7.gain_q_ref, f32[2,128]{1,0:T(2,128)S(1)} %get-tuple-element.6.gain_k_ref), custom_call_target="tpu_custom_call" | custom-call | flops 4026531840 | bytes 4194304 | tf_op jit(solution)/shard_map/head_terms/pallas_call | solution.py:233
  241.8 0.1 reshape.54
  241.9 0.1 copy.17
  242.0 0.1 copy.18
  242.1 18.7 %all_to_all.20 = f32[32,1,16]{2,1,0:T(1,128)S(1)} all-to-all(f32[32,1,16]{2,1,0:T(1,128)S(1)} %copy.18), channel_id=1, replica_groups=mesh['fsdp'=32,'sp'=16] {'fsdp'}, dimensions={0} | all-to-all | bytes 4096 | tf_op jit(solution)/shard_map/all_to_all | solution.py:278
  260.8 0.1 reduce_sum.9
  260.9 0.1 fusion
  260.9 0.6 squeeze.14
  261.6 0.6 squeeze.15
  (1 shorter events, 0.0 us)
Async XLA Ops:
  2.0 17.6 %all-to-all-start = ((f32[32,1,16]{2,1,0:T(1,128)}), f32[32,1,16]{2,1,0:T(1,128)S(1)}, u32[]{:S(2)}, u32[]{:S(2)}) async-start(f32[32,1,16]{2,1,0:T(1,128)} %broadcast_in_dim.8), calls=%async_computation | async-start | bytes 32768 | tf_op jit(solution)/shard_map/all_to_all | solution.py:267
  20.0 14.5 %copy-start.1 = (s32[16,6]{0,1:T(8,128)S(1)}, s32[16,6]{0,1:T(8,128)}, u32[]{:S(2)}) copy-start(s32[16,6]{0,1:T(8,128)} %param.14) | copy-start | bytes 1156
  20.0 199.9 %copy-start = (s32[2048]{0:T(1024)S(1)}, s32[2048]{0:T(1024)}, u32[]{:S(2)}) copy-start(s32[2048]{0:T(1024)} %order_ref.1) | copy-start | bytes 24580
  20.0 199.9 %all-to-all-start.1 = ((bf16[16,128,8,128]{3,2,1,0:T(8,128)(2,1)}), bf16[16,128,8,128]{3,2,1,0:T(8,128)(2,1)}, u32[]{:S(2)}, u32[]{:S(2)}) async-start(bf16[16,128,8,128]{3,2,1,0:T(8,128)(2,1)} %pack_tokens.1), calls=%async_computation.1 | async-start | bytes 8388608 | tf_op jit(solution)/shard_map/all_to_all | solution.py:273

commit v3 on v2

--- a/solution.py
+++ b/solution.py
@@ -81,11 +81,12 @@
     gain_q_ref,
     gain_k_ref,
     out_ref,
-    wide_ref,
+    even_ref,
+    odd_ref,
     kv_ref,
-    khat_ref,
+    kt_ref,
+    qhat_ref,
     qd_ref,
-    qe_ref,
     acc_ref,
     *stages,
 ):
@@ -97,40 +98,46 @@
     both_refs, ds_refs = stages[:heads], stages[heads:]
     acc_ref[...] = jnp.zeros_like(acc_ref)
 
-    def gather(step, carry):
-        for n in range(16):
-            place = step * 16 + n
-            token = rows_ref[order_ref[place]].astype(jnp.float32)
-            wide_ref[pl.ds(pl.multiple_of(place * rows, rows), rows), :] = token
-        return carry
-
-    lax.fori_loop(0, tokens // 16, gather, 0)
+    def gather(tile, wide_ref):
+        for n in range(TILE):
+            token = rows_ref[order_ref[tile * TILE + n]].astype(jnp.float32)
+            wide_ref[n * rows : (n + 1) * rows, :] = token
 
     def unit_rows(block):
         return block * lax.rsqrt(jnp.mean(block * block, axis=-1, keepdims=True) + 1e-06)
 
-    def arrange(tile, carry):
+    def split(block):
+        rounded = block.astype(jnp.bfloat16)
+        return rounded, (block - rounded.astype(jnp.float32)).astype(jnp.bfloat16)
+
+    def arrange(tile, wide_ref):
         for head in range(heads):
 
             def take(part):
-                return wide_ref[
-                    pl.ds(tile * TILE * rows + head * PARTS + part, TILE, stride=rows), :
-                ]
-
-            qfull = unit_rows(take(0)) * gain_q_ref[head : head + 1, :]
-            khat = unit_rows(take(1))
-            qn = qfull.astype(jnp.bfloat16)
-            kv_ref[head, tile, :, :width] = (khat * gain_k_ref[head : head + 1, :]).astype(
+                return wide_ref[pl.ds(head * PARTS + part, TILE, stride=rows), :]
+
+            qhat = unit_rows(take(0))
+            kn, rest = split(unit_rows(take(1)) * gain_k_ref[head : head + 1, :])
+            kv_ref[head, tile, :, :width] = kn
+            kv_ref[head, tile, :, width:] = take(2).astype(jnp.bfloat16)
+            kt_ref[head, tile, :width] = kn.T
+            kt_ref[head, tile, width:] = rest.T
+            qhat_ref[head, tile] = qhat
+            qd_ref[head, tile, :, :width] = (qhat * gain_q_ref[head : head + 1, :]).astype(
                 jnp.bfloat16
             )
-            kv_ref[head, tile, :, width:] = take(2).astype(jnp.bfloat16)
-            khat_ref[head, tile] = khat
-            qd_ref[head, tile, :, :width] = qn
             qd_ref[head, tile, :, width:] = take(3).astype(jnp.bfloat16)
-            qe_ref[head, tile] = (qfull - qn.astype(jnp.float32)).astype(jnp.bfloat16)
+
+    def in_order(step, carry):
+        tile = 2 * step
+        gather(tile + 1, odd_ref)
+        arrange(tile, even_ref)
+        gather(jnp.minimum(tile + 2, tiles - 1), even_ref)
+        arrange(tile + 1, odd_ref)
         return carry
 
-    lax.fori_loop(0, tiles, arrange, 0)
+    gather(0, even_ref)
+    lax.fori_loop(0, tiles // 2, in_order, 0, unroll=2)
     blank = jnp.zeros((TILE, width), jnp.bfloat16)
     spans = [slice(n * TILE, (n + 1) * TILE) for n in range(count)]
 
@@ -173,28 +180,23 @@
         factors = [factor * inverse for factor in factors]
         rowterm = jnp.zeros((8, TILE), jnp.float32)
         for span, factor in zip(spans, factors):
-            rounded = (both_ref[span, :TILE] * factor).astype(jnp.bfloat16).astype(jnp.float32)
+            probs = both_ref[span, :TILE] * factor
+            both_ref[span, :TILE] = probs
+            rounded = probs.astype(jnp.bfloat16).astype(jnp.float32)
             rowterm = rowterm + fold(rounded * both_ref[span, TILE:])
         rowterm = jnp.sum(rowterm, axis=0, keepdims=True)
-        for span, factor in zip(spans, factors):
-            probs = both_ref[span, :TILE] * factor
-            ds_ref[span, :] = (probs * (both_ref[span, TILE:] - rowterm)).astype(jnp.bfloat16)
-
-    def key_terms(head, tile):
+        for span in spans:
+            dscore = both_ref[span, :TILE] * (both_ref[span, TILE:] - rowterm)
+            ds_ref[span, :] = dscore.astype(jnp.bfloat16)
+
+    def query_terms(head, tile):
+        keys = [kt_ref[head, win_ref[tile, n]] for n in range(count)]
         sent = jnp.dot(
-            ds_refs[head][...],
-            jnp.concatenate([qd_ref[head, tile, :, :width], qe_ref[head, tile]], axis=1),
-            preferred_element_type=jnp.float32,
+            jnp.concatenate(keys, axis=1), ds_refs[head][...], preferred_element_type=jnp.float32
         )
-        sum_q, sum_k = acc_ref[0, head], acc_ref[1, head]
-        for n, span in enumerate(spans):
-            pick = win_ref[tile, n]
-            dkey, rest = sent[span, :width], sent[span, width:]
-            kn = kv_ref[head, pick, :, :width].astype(jnp.float32)
-            sum_q = sum_q + fold(kn * (dkey + rest))
-            sum_k = sum_k + fold(khat_ref[head, pick] * dkey)
-        acc_ref[0, head] = sum_q
-        acc_ref[1, head] = sum_k
+        dqn, rest = sent[:width].T, sent[width:].T
+        acc_ref[0, head] += fold(dqn * qhat_ref[head, tile])
+        acc_ref[1, head] += fold((dqn + rest) * qd_ref[head, tile, :, :width].astype(jnp.float32))
 
     last = heads - 1
     for ds_ref in ds_refs:
@@ -203,25 +205,25 @@
 
     def attend(tile, carry):
         for head in range(heads):
+            softmax_grad(head)
             if head < last:
                 products(head + 1, tile)
             else:
                 products(0, jnp.minimum(tile + 1, tiles - 1))
-            softmax_grad(head)
             if head > 0:
-                key_terms(head - 1, tile)
+                query_terms(head - 1, tile)
             else:
-                key_terms(last, jnp.maximum(tile - 1, 0))
+                query_terms(last, jnp.maximum(tile - 1, 0))
         return carry
 
-    lax.fori_loop(0, tiles, attend, 0)
-    key_terms(last, tiles - 1)
+    lax.fori_loop(0, tiles, attend, 0, unroll=2)
+    query_terms(last, tiles - 1)
     for head in range(heads):
         row = slice(head, head + 1)
         sums_q = jnp.sum(acc_ref[0, head], axis=0, keepdims=True)
         sums_k = jnp.sum(acc_ref[1, head], axis=0, keepdims=True)
-        out_ref[0, row, :] = sums_q * scale / gain_q_ref[row, :]
-        out_ref[1, row, :] = sums_k * scale
+        out_ref[0, row, :] = sums_q * scale
+        out_ref[1, row, :] = sums_k * scale / gain_k_ref[row, :]
 
 
 def head_terms(rows, order, gain_q, gain_k, windows):
@@ -236,11 +238,12 @@
         in_specs=[smem, smem, vmem, vmem, vmem],
         out_specs=vmem,
         scratch_shapes=[
-            pltpu.VMEM((tokens * heads * PARTS, width), jnp.float32),
+            pltpu.VMEM((TILE * heads * PARTS, width), jnp.float32),
+            pltpu.VMEM((TILE * heads * PARTS, width), jnp.float32),
             pltpu.VMEM((heads, tiles, TILE, 2 * width), jnp.bfloat16),
+            pltpu.VMEM((heads, tiles, 2 * width, TILE), jnp.bfloat16),
             pltpu.VMEM((heads, tiles, TILE, width), jnp.float32),
             pltpu.VMEM((heads, tiles, TILE, 2 * width), jnp.bfloat16),
-            pltpu.VMEM((heads, tiles, TILE, width), jnp.bfloat16),
             pltpu.VMEM((2, heads, 8, width), jnp.float32),
             *[pltpu.VMEM((count * TILE, 2 * TILE), jnp.float32)] * heads,
             *[pltpu.VMEM((count * TILE, TILE), jnp.bfloat16)] * heads,
@@ -262,15 +265,10 @@
     heads, own = gain_q.shape
     width = own * spread
 
-    shares = jnp.stack([gain_q, gain_k]).reshape(1, 2 * heads * own)
-    shares = jnp.broadcast_to(shares, (spread, 2 * heads * own))
-    shares = lax.all_to_all(shares, "fsdp", split_axis=0, concat_axis=0, tiled=True)
-    gains = jnp.transpose(shares.reshape(spread, 2, heads, own), (1, 2, 0, 3))
-    gains = gains.reshape(2, heads, width)
-
     packed = pack((query, key, value, cotangent), groups, heads, width)
-    packed, gains = lax.optimization_barrier((packed, gains))
+    packed, gain_q, gain_k = lax.optimization_barrier((packed, gain_q, gain_k))
     rows = lax.all_to_all(packed, "sp", split_axis=0, concat_axis=0, tiled=True)
+    gains = gather_gains(jnp.stack([gain_q, gain_k]), spread)
     rows = rows.reshape(groups * tokens, heads * PARTS, width)
     terms = head_terms(rows, order, gains[0], gains[1], windows)
     terms = jnp.transpose(terms.reshape(2, heads, spread, own), (2, 0, 1, 3))
@@ -278,6 +276,24 @@
     arrived = lax.all_to_all(terms, "fsdp", split_axis=0, concat_axis=0, tiled=True)
     sums = jnp.sum(arrived, axis=0).reshape(2, heads, own)
     return (sums[0], sums[1])
+
+
+def gather_gains(share, spread):
+    def from_offset(block, offset):
+        return lax.ppermute(block, "fsdp", [(i, i ^ offset) for i in range(spread)])
+
+    shares, offsets = share[None], [0]
+    for step in ((1,), (8,), (16,), (2, 4, 6)):
+        step = [offset for offset in step if offset < spread]
+        parts = [shares] + [from_offset(shares, offset) for offset in step]
+        offsets = [own ^ offset for offset in [0] + step for own in offsets]
+        shares = jnp.concatenate(parts, axis=0)
+    places = jnp.arange(spread, dtype=jnp.int32)[:, None] ^ lax.axis_index("fsdp")
+    onehot = (places == jnp.array(offsets, jnp.int32)[None, :]).astype(jnp.float32)
+    kinds, heads, own = share.shape
+    picked = jnp.sum(onehot[:, :, None] * shares.reshape(1, spread, kinds * heads * own), axis=1)
+    gains = jnp.transpose(picked.reshape(spread, kinds, heads, own), (1, 2, 0, 3))
+    return gains.reshape(kinds, heads, spread * own)
 
 
 def solution(mesh):

time: 266 us -> 251 us (0.944); the launches traced: 262 us -> 250 us
  waiting for transfers between devices: 188 us -> 159 us
  starting transfers between devices: 24.8 us -> 38.5 us
  blocking collectives: 18.7 us -> 24.6 us
  Pallas kernels: 26.6 us -> 23.5 us
    all_to_all x1, waiting for transfers between devices: 185 us -> 0.01 us  [shards(): rows = lax.all_to_all(packed, 'sp', split_axis=0, concat_axis=0, tiled=True)]
    ppermute x0 -> x6, waiting for transfers between devices: none -> 159 us  [from_offset(): return lax.ppermute(block, 'fsdp', [(i, i ^ offset) for i in range(spread)])]
    ppermute x0 -> x6, starting transfers between devices: none -> 19.9 us  [from_offset(): return lax.ppermute(block, 'fsdp', [(i, i ^ offset) for i in range(spread)])]
    all_to_all x1 -> x0, starting transfers between devices: 10.3 us -> none  [shards(): lax.all_to_all(shares, 'fsdp', split_axis=0, concat_axis=0, tiled=True)]
    all_to_all x1, blocking collectives: 18.7 us -> 24.6 us  [shards(): lax.all_to_all(terms, 'fsdp', split_axis=0, concat_axis=0, tiled=True)]
    all_to_all x1, starting transfers between devices: 14.5 us -> 18.6 us  [shards(): rows = lax.all_to_all(packed, 'sp', split_axis=0, concat_axis=0, tiled=True)]
    pallas_call x1, Pallas kernels: 21.9 us -> 18.7 us  [head_terms(): pl.pallas_call(terms_kernel, out_shape=jax.ShapeDtypeStruct((2, heads, wi...]
  transfers between devices with their start and end apart: 2 -> 7, of which waited for: 2 -> 4; matrix products, arithmetic and copies ran while one was open for 0% -> 1% of each run, Pallas kernels for 2% -> 0%
where the time goes in v3:
time: 251 us; the launch traced here: 250 us
  waiting for transfers between devices  159 us (63%)
  starting transfers between devices  38.5 us (15%)
  blocking collectives  24.6 us (10%)
  Pallas kernels  23.5 us (9%)
  local copies, waits for them, and re-layouts  3.01 us (1%)
    ppermute x6, waiting for transfers between devices, from_offset(): return lax.ppermute(block, 'fsdp', [(i, i ^ offset) for i in range(spread)])  159 us
    all_to_all x1, blocking collectives, shards(): lax.all_to_all(terms, 'fsdp', split_axis=0, concat_axis=0, tiled=True)  24.6 us
    ppermute x6, starting transfers between devices, from_offset(): return lax.ppermute(block, 'fsdp', [(i, i ^ offset) for i in range(spread)])  19.9 us
    pallas_call x1, Pallas kernels, head_terms(): pl.pallas_call(terms_kernel, out_shape=jax.ShapeDtypeStruct((2, heads, wi...  18.7 us
    all_to_all x1, starting transfers between devices, shards(): rows = lax.all_to_all(packed, 'sp', split_axis=0, concat_axis=0, tiled=True)  18.6 us
  transfers between devices with their start and end apart: 7, of which 4 were waited for; matrix products, arithmetic and copies ran while one was open for 1% of the time, Pallas kernels for 0%

profile of v3, /device:TPU:1, one launch (start us, length us, event | category | flops | bytes accessed | tf_op | source)
XLA Modules:
  0.0 250.1 jit_solution(16301404295607595782)
XLA Ops:
  0.6 4.8 %pack_tokens.1 = bf16[16,128,8,128]{3,2,1,0:T(8,128)(2,1)} custom-call(bf16[1,128,4096]{2,1,0:T(8,128)(2,1)} %refs_0_.1, bf16[1,128,4096]{2,1,0:T(8,128)(2,1)} %refs_1_.1, bf16[1,128,4096]{2,1,0:T(8,128)(2,1)} %refs_2_.1, bf16[1,128,4096]{2,1,0:T(8,128)(2,1)} %refs_3_.1), custom_call_target="tpu_custom_call" | custom-call | bytes 8388608 | tf_op jit(solution)/shard_map/pack_tokens/pallas_call | solution.py:57
  5.5 18.6 %all-to-all-start = ((bf16[16,128,8,128]{3,2,1,0:T(8,128)(2,1)}), bf16[16,128,8,128]{3,2,1,0:T(8,128)(2,1)}, u32[]{:S(2)}, u32[]{:S(2)}) async-start(bf16[16,128,8,128]{3,2,1,0:T(8,128)(2,1)} %pack_tokens.1), calls=%async_computation | async-start | bytes 8388608 | tf_op jit(solution)/shard_map/all_to_all | solution.py:270
  24.1 2.9 %collective-permute-start = (f32[1,2,2,4]{3,2,1,0:T(2,128)S(1)}, f32[1,2,2,4]{3,2,1,0:T(2,128)S(1)}, u32[]{:S(2)}, u32[]{:S(2)}) collective-permute-start(f32[1,2,2,4]{3,2,1,0:T(2,128)S(1)} %get-tuple-element.10), channel_id=1, source_target_pairs={{0,16},{16,0},{32,48},{48,32},{64,80},{80,64},{96,112},{112,96},{1... | collective-permute-start | bytes 200 | tf_op jit(solution)/shard_map/ppermute | solution.py:283
  26.9 0.8 collective-permute-done
  27.7 3.1 %collective-permute-start.1 = (f32[2,2,2,4]{3,2,1,0:T(2,128)S(1)}, f32[2,2,2,4]{3,2,1,0:T(2,128)S(1)}, u32[]{:S(2)}, u32[]{:S(2)}) collective-permute-start(f32[2,2,2,4]{3,2,1,0:T(2,128)S(1)} %pad_maximum_fusion.2), channel_id=1, source_target_pairs={{0,128},{16,144},{32,160},{48,176},{64,192},{80,208},{96,224},{112... | collective-permute-start | bytes 392 | tf_op jit(solution)/shard_map/ppermute | solution.py:283
  30.9 1.6 collective-permute-done.1
  32.5 4.6 %collective-permute-start.2 = (f32[4,2,2,4]{3,2,1,0:T(2,128)S(1)}, f32[4,2,2,4]{3,2,1,0:T(2,128)S(1)}, u32[]{:S(2)}, u32[]{:S(2)}) collective-permute-start(f32[4,2,2,4]{3,2,1,0:T(2,128)S(1)} %pad_maximum_fusion.1), channel_id=1, source_target_pairs={{0,256},{16,272},{32,288},{48,304},{64,320},{80,336},{96,352},{112... | collective-permute-start | bytes 776 | tf_op jit(solution)/shard_map/ppermute | solution.py:283
  37.2 1.6 collective-permute-done.2
  38.8 2.6 %collective-permute-start.3 = (f32[8,2,2,4]{3,2,1,0:T(2,128)S(1)}, f32[8,2,2,4]{3,2,1,0:T(2,128)S(1)}, u32[]{:S(2)}, u32[]{:S(2)}) collective-permute-start(f32[8,2,2,4]{3,2,1,0:T(2,128)S(1)} %pad_maximum_fusion), channel_id=1, source_target_pairs={{0,32},{16,48},{32,0},{48,16},{64,96},{80,112},{96,64},{112,80},{1... | collective-permute-start | bytes 1544 | tf_op jit(solution)/shard_map/ppermute | solution.py:283
  41.5 3.1 %collective-permute-start.4 = (f32[8,2,2,4]{3,2,1,0:T(2,128)S(1)}, f32[8,2,2,4]{3,2,1,0:T(2,128)S(1)}, u32[]{:S(2)}, u32[]{:S(2)}) collective-permute-start(f32[8,2,2,4]{3,2,1,0:T(2,128)S(1)} %pad_maximum_fusion), channel_id=1, source_target_pairs={{0,64},{16,80},{32,96},{48,112},{64,0},{80,16},{96,32},{112,48},{1... | collective-permute-start | bytes 1544 | tf_op jit(solution)/shard_map/ppermute | solution.py:283
  44.6 3.5 %collective-permute-start.5 = (f32[8,2,2,4]{3,2,1,0:T(2,128)S(1)}, f32[8,2,2,4]{3,2,1,0:T(2,128)S(1)}, u32[]{:S(2)}, u32[]{:S(2)}) collective-permute-start(f32[8,2,2,4]{3,2,1,0:T(2,128)S(1)} %pad_maximum_fusion), channel_id=1, source_target_pairs={{0,96},{16,112},{32,64},{48,80},{64,32},{80,48},{96,0},{112,16},{1... | collective-permute-start | bytes 1544 | tf_op jit(solution)/shard_map/ppermute | solution.py:283
  48.2 0.1 concatenate.41
  48.2 0.1 copy.55.win_ref
  48.4 0.1 copy.58
  48.5 0.1 copy.59
  48.6 155.3 %collective-permute-done.3 = f32[8,2,2,4]{3,2,1,0:T(2,128)S(1)} collective-permute-done((f32[8,2,2,4]{3,2,1,0:T(2,128)S(1)}, f32[8,2,2,4]{3,2,1,0:T(2,128)S(1)}, u32[]{:S(2)}, u32[]{:S(2)}) %collective-permute-start.3) | collective-permute-done | bytes 544 | tf_op jit(solution)/shard_map/ppermute | solution.py:283
  204.0 0.1 copy.45
  204.1 0.1 copy.46
  204.2 0.1 copy.47
  204.3 0.1 concatenate.40
  204.4 0.1 multiply_reduce_fusion
  204.6 0.1 copy.53
  204.7 0.1 squeeze.12.gain_q_ref
  204.8 0.1 copy.54
  204.9 0.1 squeeze.13.gain_k_ref
  205.0 18.7 %head_terms.1 = f32[2,2,128]{2,1,0:T(2,128)S(1)} custom-call(s32[16,6]{1,0:T(8,128)S(1)} %copy.55.win_ref, s32[2048]{0:T(1024)S(1)} %copy-done, bf16[2048,8,128]{2,1,0:T(8,128)(2,1)} %bitcast.rows_ref, f32[2,128]{1,0:T(2,128)S(1)} %squeeze.12.gain_q_ref, f32[2,128]{1,0:T(2,128)S(1)} %squeeze.13.gain_k_ref), custom_call_target="tpu_custom_call" | custom-call | flops 4026531840 | bytes 4194304 | tf_op jit(solution)/shard_map/head_terms/pallas_call | solution.py:235
  223.8 0.1 reshape.86
  223.9 0.1 copy.56
  224.0 0.1 copy.57
  224.1 24.6 %all_to_all.14 = f32[32,1,16]{2,1,0:T(1,128)S(1)} all-to-all(f32[32,1,16]{2,1,0:T(1,128)S(1)} %copy.57), channel_id=1, replica_groups=mesh['fsdp'=32,'sp'=16] {'fsdp'}, dimensions={0} | all-to-all | bytes 4096 | tf_op jit(solution)/shard_map/all_to_all | solution.py:276
  248.8 0.6 squeeze.14
  249.5 0.6 squeeze.15
  (24 shorter events, 0.4 us)
Async XLA Ops:
  5.4 18.6 %copy-start.2 = (f32[2,4]{1,0:T(2,128)S(1)}, f32[2,4]{1,0:T(2,128)}, u32[]{:S(2)}) copy-start(f32[2,4]{1,0:T(2,128)} %param.14) | copy-start | bytes 100
  5.4 18.6 %copy-start.3 = (f32[2,4]{1,0:T(2,128)S(1)}, f32[2,4]{1,0:T(2,128)}, u32[]{:S(2)}) copy-start(f32[2,4]{1,0:T(2,128)} %param.13) | copy-start | bytes 100
  5.4 36.0 %copy-start.4 = (s32[32]{0:T(128)S(1)}, s32[32]{0:T(128)}, u32[]{:S(2)}) copy-start(s32[32]{0:T(128)} %constant.10.clone) | copy-start | bytes 388
  5.4 42.8 %copy-start.1 = (s32[16,6]{0,1:T(8,128)S(1)}, s32[16,6]{0,1:T(8,128)}, u32[]{:S(2)}) copy-start(s32[16,6]{0,1:T(8,128)} %param.15) | copy-start | bytes 1156
  5.4 199.6 %copy-start = (s32[2048]{0:T(1024)S(1)}, s32[2048]{0:T(1024)}, u32[]{:S(2)}) copy-start(s32[2048]{0:T(1024)} %order_ref.1) | copy-start | bytes 24580
  5.5 199.6 %all-to-all-start = ((bf16[16,128,8,128]{3,2,1,0:T(8,128)(2,1)}), bf16[16,128,8,128]{3,2,1,0:T(8,128)(2,1)}, u32[]{:S(2)}, u32[]{:S(2)}) async-start(bf16[16,128,8,128]{3,2,1,0:T(8,128)(2,1)} %pack_tokens.1), calls=%async_computation | async-start | bytes 8388608 | tf_op jit(solution)/shard_map/all_to_all | solution.py:270
  24.1 3.7 %collective-permute-start = (f32[1,2,2,4]{3,2,1,0:T(2,128)S(1)}, f32[1,2,2,4]{3,2,1,0:T(2,128)S(1)}, u32[]{:S(2)}, u32[]{:S(2)}) collective-permute-start(f32[1,2,2,4]{3,2,1,0:T(2,128)S(1)} %get-tuple-element.10), channel_id=1, source_target_pairs={{0,16},{16,0},{32,48},{48,32},{64,80},{80,64},{96,112},{112,96},{1... | collective-permute-start | bytes 200 | tf_op jit(solution)/shard_map/ppermute | solution.py:283
  27.7 4.7 %collective-permute-start.1 = (f32[2,2,2,4]{3,2,1,0:T(2,128)S(1)}, f32[2,2,2,4]{3,2,1,0:T(2,128)S(1)}, u32[]{:S(2)}, u32[]{:S(2)}) collective-permute-start(f32[2,2,2,4]{3,2,1,0:T(2,128)S(1)} %pad_maximum_fusion.2), channel_id=1, source_target_pairs={{0,128},{16,144},{32,160},{48,176},{64,192},{80,208},{96,224},{112... | collective-permute-start | bytes 392 | tf_op jit(solution)/shard_map/ppermute | solution.py:283
  32.5 6.3 %collective-permute-start.2 = (f32[4,2,2,4]{3,2,1,0:T(2,128)S(1)}, f32[4,2,2,4]{3,2,1,0:T(2,128)S(1)}, u32[]{:S(2)}, u32[]{:S(2)}) collective-permute-start(f32[4,2,2,4]{3,2,1,0:T(2,128)S(1)} %pad_maximum_fusion.1), channel_id=1, source_target_pairs={{0,256},{16,272},{32,288},{48,304},{64,320},{80,336},{96,352},{112... | collective-permute-start | bytes 776 | tf_op jit(solution)/shard_map/ppermute | solution.py:283
  38.8 165.2 %collective-permute-start.3 = (f32[8,2,2,4]{3,2,1,0:T(2,128)S(1)}, f32[8,2,2,4]{3,2,1,0:T(2,128)S(1)}, u32[]{:S(2)}, u32[]{:S(2)}) collective-permute-start(f32[8,2,2,4]{3,2,1,0:T(2,128)S(1)} %pad_maximum_fusion), channel_id=1, source_target_pairs={{0,32},{16,48},{32,0},{48,16},{64,96},{80,112},{96,64},{112,80},{1... | collective-permute-start | bytes 1544 | tf_op jit(solution)/shard_map/ppermute | solution.py:283
  41.5 162.5 %collective-permute-start.4 = (f32[8,2,2,4]{3,2,1,0:T(2,128)S(1)}, f32[8,2,2,4]{3,2,1,0:T(2,128)S(1)}, u32[]{:S(2)}, u32[]{:S(2)}) collective-permute-start(f32[8,2,2,4]{3,2,1,0:T(2,128)S(1)} %pad_maximum_fusion), channel_id=1, source_target_pairs={{0,64},{16,80},{32,96},{48,112},{64,0},{80,16},{96,32},{112,48},{1... | collective-permute-start | bytes 1544 | tf_op jit(solution)/shard_map/ppermute | solution.py:283
  44.6 159.5 %collective-permute-start.5 = (f32[8,2,2,4]{3,2,1,0:T(2,128)S(1)}, f32[8,2,2,4]{3,2,1,0:T(2,128)S(1)}, u32[]{:S(2)}, u32[]{:S(2)}) collective-permute-start(f32[8,2,2,4]{3,2,1,0:T(2,128)S(1)} %pad_maximum_fusion), channel_id=1, source_target_pairs={{0,96},{16,112},{32,64},{48,80},{64,32},{80,48},{96,0},{112,16},{1... | collective-permute-start | bytes 1544 | tf_op jit(solution)/shard_map/ppermute | solution.py:283

commit v4 on v3

v4 whole, which is shorter than its diff:
```python
import functools

import jax
import jax.numpy as jnp
from jax import lax
from jax.experimental import pallas as pl
from jax.experimental.pallas import tpu as pltpu
from jax.sharding import PartitionSpec as P

TILE = 128
LOG2E = 1.4426950408889634
PARTS = 4
INNER = 4


def pack(arrays, head, groups, heads, width, axis=None):
    tokens, flat = arrays[0].shape[1:]
    rows = tokens * PARTS
    chunks = 4
    span = flat // chunks

    def body(*refs):
        ins, out_ref = refs[:PARTS], refs[PARTS]
        held_ref, ready_ref, wide_ref, in_sems, out_sems = refs[PARTS + 1 :]
        arrivals = []
        for chunk in range(chunks):
            lanes = slice(chunk * span, (chunk + 1) * span)
            arrivals.append(
                [
                    pltpu.make_async_copy(
                        ins[part].at[0, :, lanes],
                        held_ref.at[part, :, lanes],
                        in_sems.at[chunk, part],
                    )
                    for part in range(PARTS)
                ]
            )
            for copy in arrivals[-1]:
                copy.start()
        leaving = []
        for dest in range(groups):
            if dest % (groups // chunks) == 0:
                for copy in arrivals[dest // (groups // chunks)]:
                    copy.wait()
            start = (dest * heads + head) * width
            for part in range(PARTS):
                block = held_ref[part, :, start : start + width].astype(jnp.float32)
                wide_ref[dest % 2, pl.ds(part, tokens, stride=PARTS), :] = block
            ready_ref[dest] = wide_ref[dest % 2].astype(jnp.bfloat16)
            place = dest if axis is None else dest ^ lax.axis_index(axis)
            leaving.append(
                pltpu.make_async_copy(ready_ref.at[dest], out_ref.at[place], out_sems.at[dest])
            )
            leaving[-1].start()
        for copy in leaving:
            copy.wait()

    return pl.pallas_call(
        body,
        out_shape=jax.ShapeDtypeStruct((groups, rows, width), jnp.bfloat16),
        in_specs=[pl.BlockSpec(memory_space=pl.ANY)] * PARTS,
        out_specs=pl.BlockSpec(memory_space=pl.ANY),
        scratch_shapes=[
            pltpu.VMEM((PARTS, tokens, flat), jnp.bfloat16),
            pltpu.VMEM((groups, rows, width), jnp.bfloat16),
            pltpu.VMEM((2, rows, width), jnp.float32),
            pltpu.SemaphoreType.DMA((chunks, PARTS)),
            pltpu.SemaphoreType.DMA((groups,)),
        ],
        compiler_params=pltpu.CompilerParams(vmem_limit_bytes=56 * 2**20),
        cost_estimate=pl.CostEstimate(
            flops=0, bytes_accessed=6 * groups * rows * width, transcendentals=0
        ),
        name="pack_head",
    )(*arrays)


def terms_kernel(head, inputs, win_ref, starts_ref, *refs):
    row_refs, (gain_q_ref, gain_k_ref, out_ref) = refs[:inputs], refs[inputs : inputs + 3]
    held_ref, sems, plain_ref, even_ref, odd_ref = refs[inputs + 3 : inputs + 8]
    kv_ref, kt_ref, qhat_ref, qd_ref, acc_ref = refs[inputs + 8 : inputs + 13]
    both_refs, ds_refs = refs[inputs + 13 : inputs + 15], refs[inputs + 15 :]
    tiles, count = win_ref.shape
    width = gain_q_ref.shape[1]
    scale = width ** (-0.5)
    blocks = held_ref.shape[0]
    rows = held_ref.shape[1]
    pieces = sems.shape[0]
    gain_q, gain_k = gain_q_ref[head : head + 1, :], gain_k_ref[head : head + 1, :]

    each = blocks // pieces
    copies = []
    for piece in range(pieces):
        ref = row_refs[piece * inputs // pieces]
        first = piece * each % ref.shape[0]
        copies.append(
            pltpu.make_async_copy(
                ref.at[first : first + each],
                held_ref.at[piece * each : (piece + 1) * each],
                sems.at[piece],
            )
        )
        copies[-1].start()
    acc_ref[...] = jnp.zeros_like(acc_ref)
    for ds_ref in ds_refs:
        ds_ref[...] = jnp.zeros_like(ds_ref)
    for piece in range(pieces):
        copies[piece].wait()
        for block in range(piece * each, (piece + 1) * each):
            plain_ref[block * rows : (block + 1) * rows, :] = held_ref[block].astype(jnp.float32)

    def gather(tile, wide_ref):
        for n in range(TILE):
            start = pl.multiple_of(starts_ref[tile * TILE + n], PARTS)
            wide_ref[n * PARTS : (n + 1) * PARTS, :] = plain_ref[pl.ds(start, PARTS), :]

    def unit_rows(block):
        return block * lax.rsqrt(jnp.mean(block * block, axis=-1, keepdims=True) + 1e-06)

    def split(block):
        rounded = block.astype(jnp.bfloat16)
        return rounded, (block - rounded.astype(jnp.float32)).astype(jnp.bfloat16)

    def arrange(tile, wide_ref):
        def take(part):
            return wide_ref[pl.ds(part, TILE, stride=PARTS), :]

        qhat = unit_rows(take(0))
        kn, rest = split(unit_rows(take(1)) * gain_k)
        kv_ref[tile, :, :width] = kn
        kv_ref[tile, :, width:] = take(2).astype(jnp.bfloat16)
        kt_ref[tile, :width] = kn.T
        kt_ref[tile, width:] = rest.T
        qhat_ref[tile] = qhat
        qd_ref[tile, :, :width] = (qhat * gain_q).astype(jnp.bfloat16)
        qd_ref[tile, :, width:] = take(3).astype(jnp.bfloat16)

    def in_order(step, carry):
        tile = 2 * step
        gather(tile + 1, odd_ref)
        arrange(tile, even_ref)
        gather(jnp.minimum(tile + 2, tiles - 1), even_ref)
        arrange(tile + 1, odd_ref)
        return carry

    gather(0, even_ref)
    lax.fori_loop(0, tiles // 2, in_order, 0, unroll=2)
    blank = jnp.zeros((TILE, width), jnp.bfloat16)
    spans = [slice(n * TILE, (n + 1) * TILE) for n in range(count)]

    def fold(block):
        return jnp.sum(block.reshape(-1, 8, width), axis=0)

    def products(slot, tile):
        qn, grad = qd_ref[tile, :, :width], qd_ref[tile, :, width:]
        both_refs[slot][...] = lax.dot_general(
            jnp.concatenate([kv_ref[win_ref[tile, n]] for n in range(count)], axis=0),
            jnp.concatenate(
                [
                    jnp.concatenate([qn, blank], axis=1),
                    jnp.concatenate([blank, grad], axis=1),
                ],
                axis=0,
            ),
            (((1,), (1,)), ((), ())),
            preferred_element_type=jnp.float32,
        )

    def softmax_grad(slot):
        both_ref, ds_ref = both_refs[slot], ds_refs[slot]
        tops, sums = [], []
        for span in spans:
            scores = both_ref[span, :TILE]
            top = jnp.max(scores, axis=0, keepdims=True)
            weights = jnp.exp2((scores - top) * (scale * LOG2E))
            both_ref[span, :TILE] = weights
            tops.append(top)
            sums.append(jnp.sum(weights, axis=0, keepdims=True))
        highest = tops[0]
        for top in tops[1:]:
            highest = jnp.maximum(highest, top)
        factors = [jnp.exp2((top - highest) * (scale * LOG2E)) for top in tops]
        total = sums[0] * factors[0]
        for n in range(1, count):
            total = total + sums[n] * factors[n]
        inverse = 1.0 / total
        factors = [factor * inverse for factor in factors]
        rowterm = jnp.zeros((8, TILE), jnp.float32)
        for span, factor in zip(spans, factors):
            probs = both_ref[span, :TILE] * factor
            both_ref[span, :TILE] = probs
            rounded = probs.astype(jnp.bfloat16).astype(jnp.float32)
            rowterm = rowterm + fold(rounded * both_ref[span, TILE:])
        rowterm = jnp.sum(rowterm, axis=0, keepdims=True)
        for span in spans:
            dscore = both_ref[span, :TILE] * (both_ref[span, TILE:] - rowterm)
            ds_ref[span, :] = dscore.astype(jnp.bfloat16)

    def query_terms(slot, tile):
        keys = [kt_ref[win_ref[tile, n]] for n in range(count)]
        sent = jnp.dot(
            jnp.concatenate(keys, axis=1), ds_refs[slot][...], preferred_element_type=jnp.float32
        )
        dqn, rest = sent[:width].T, sent[width:].T
        acc_ref[0] += fold(dqn * qhat_ref[tile])
        acc_ref[1] += fold((dqn + rest) * qd_ref[tile, :, :width].astype(jnp.float32))

    products(0, 0)

    def attend(step, carry):
        for slot in range(2):
            tile = 2 * step + slot
            softmax_grad(slot)
            products(1 - slot, jnp.minimum(tile + 1, tiles - 1))
            query_terms(1 - slot, jnp.maximum(tile - 1, 0))
        return carry

    lax.fori_loop(0, tiles // 2, attend, 0, unroll=2)
    query_terms(1, tiles - 1)
    out_ref[0:1, :] = jnp.sum(acc_ref[0], axis=0, keepdims=True) * scale
    out_ref[1:2, :] = jnp.sum(acc_ref[1], axis=0, keepdims=True) * scale / gain_k


def head_terms(rows, starts, gain_q, gain_k, windows, head):
    tiles, count = windows.shape
    width = gain_q.shape[1]
    depth = rows[0].shape[1]
    blocks = sum(block.shape[0] for block in rows)
    tokens = tiles * TILE
    vmem = pl.BlockSpec(memory_space=pltpu.VMEM)
    smem = pl.BlockSpec(memory_space=pltpu.SMEM)
    anywhere = pl.BlockSpec(memory_space=pl.ANY)
    return pl.pallas_call(
        functools.partial(terms_kernel, head, len(rows)),
        out_shape=jax.ShapeDtypeStruct((2, width), jnp.float32),
        in_specs=[smem, smem] + [anywhere] * len(rows) + [vmem, vmem],
        out_specs=vmem,
        scratch_shapes=[
            pltpu.VMEM((blocks, depth, width), jnp.bfloat16),
            pltpu.SemaphoreType.DMA((4,)),
            pltpu.VMEM((blocks * depth, width), jnp.float32),
            pltpu.VMEM((TILE * PARTS, width), jnp.float32),
            pltpu.VMEM((TILE * PARTS, width), jnp.float32),
            pltpu.VMEM((tiles, TILE, 2 * width), jnp.bfloat16),
            pltpu.VMEM((tiles, 2 * width, TILE), jnp.bfloat16),
            pltpu.VMEM((tiles, TILE, width), jnp.float32),
            pltpu.VMEM((tiles, TILE, 2 * width), jnp.bfloat16),
            pltpu.VMEM((2, 8, width), jnp.float32),
            *[pltpu.VMEM((count * TILE, 2 * TILE), jnp.float32)] * 2,
            *[pltpu.VMEM((count * TILE, TILE), jnp.bfloat16)] * 2,
        ],
        compiler_params=pltpu.CompilerParams(vmem_limit_bytes=28 * 2**20),
        cost_estimate=pl.CostEstimate(
            flops=10 * tokens * count * TILE * width,
            bytes_accessed=blocks * depth * width * 2,
            transcendentals=tokens * count * TILE,
        ),
        name="head_terms",
    )(windows, starts, *rows, gain_q, gain_k)


def shards(query, key, value, cotangent, gain_q, gain_k, windows, order):
    groups = lax.axis_size("sp")
    spread = lax.axis_size("fsdp")
    tokens = query.shape[1]
    heads, own = gain_q.shape
    width = own * spread

    arrays = (query, key, value, cotangent)
    first = pack(arrays, 0, groups, heads, width)
    first, gain_q, gain_k, *arrays = lax.optimization_barrier((first, gain_q, gain_k, *arrays))
    first = lax.all_to_all(first, "sp", split_axis=0, concat_axis=0, tiled=True)
    shares, offsets = gather_shares(jnp.stack([gain_q, gain_k])[None], [0], ((1,), (8,), (16,)))
    second = along_y(pack(arrays, 1, groups, heads, width, "sp"))
    shares, *second = lax.optimization_barrier((shares, *second))
    shares, offsets = gather_shares(shares, offsets, ((2, 4, 6),))
    gains = in_channel_order(shares, jnp.array(offsets, jnp.int32), spread)
    second, starts = along_z(second, order, tokens)
    terms = [head_terms([first], order * PARTS, gains[0], gains[1], windows, 0)]
    starts, terms[0] = lax.optimization_barrier((starts, terms[0]))
    terms.append(head_terms(second, starts, gains[0], gains[1], windows, 1))
    terms = jnp.transpose(jnp.stack(terms).reshape(heads, 2, spread, own), (2, 1, 0, 3))
    terms = terms.reshape(spread, 2 * heads * own)
    arrived = lax.all_to_all(terms, "fsdp", split_axis=0, concat_axis=0, tiled=True)
    sums = jnp.sum(arrived, axis=0).reshape(2, heads, own)
    return (sums[0], sums[1])


def permute(block, axis, offset):
    pairs = [(i, i ^ offset) for i in range(lax.axis_size(axis))]
    return lax.ppermute(block, axis, pairs)


def along_y(packed):
    columns = [packed[:INNER]]
    for offset in range(INNER, packed.shape[0], INNER):
        columns.append(permute(packed[offset : offset + INNER], "sp", offset))
    return [jnp.stack([column[n] for column in columns]) for n in range(INNER)]


def along_z(blocks, order, tokens):
    outer = blocks[0].shape[0]
    blocks = [blocks[0]] + [permute(blocks[n], "sp", n) for n in range(1, INNER)]
    away = (order // tokens) ^ lax.axis_index("sp")
    block = (away % INNER) * outer + away // INNER
    return blocks, (block * tokens + order % tokens) * PARTS


def gather_shares(shares, offsets, steps):
    for step in steps:
        parts = [shares] + [permute(shares, "fsdp", offset) for offset in step]
        offsets = [own ^ offset for offset in [0] + list(step) for own in offsets]
        shares = jnp.concatenate(parts, axis=0)
    return shares, offsets


def in_channel_order(shares, offsets, spread):
    places = jnp.arange(spread, dtype=jnp.int32)[:, None] ^ lax.axis_index("fsdp")
    onehot = (places == offsets[None, :]).astype(jnp.float32)
    kinds, heads, own = shares.shape[1:]
    picked = jnp.sum(onehot[:, :, None] * shares.reshape(1, spread, kinds * heads * own), axis=1)
    gains = jnp.transpose(picked.reshape(spread, kinds, heads, own), (1, 2, 0, 3))
    return gains.reshape(kinds, heads, spread * own)


def solution(mesh):
    placed = (
        P("fsdp", "sp", None),
        P("fsdp", "sp", None),
        P("fsdp", "sp", None),
        P("fsdp", "sp", None),
        P("sp", "fsdp"),
        P("sp", "fsdp"),
        P(),
        P(),
    )
    return jax.shard_map(
        shards,
        mesh=mesh,
        in_specs=placed,
        out_specs=(P("sp", "fsdp"), P("sp", "fsdp")),
        check_vma=False,
    )
```

time: 251 us -> 241 us (0.960)
  waiting for transfers between devices: 159 us -> 105 us
  starting transfers between devices: 38.5 us -> 70.4 us
  other arithmetic: 0.3 us -> 6.95 us
  local copies, waits for them, and re-layouts: 3.01 us -> 9.11 us
  blocking collectives: 24.6 us -> 20.2 us
  Pallas kernels: 23.5 us -> 27.9 us
    ppermute x6 -> x12, waiting for transfers between devices: 159 us -> 105 us  [permute(): return lax.ppermute(block, axis, pairs)]
    ppermute x6 -> x12, starting transfers between devices: 19.9 us -> 52 us  [permute(): return lax.ppermute(block, axis, pairs)]
    slice x3 -> x8, local copies, waits for them, and re-layouts: 0.2 us -> 5.76 us  [the longest x4 2.98 us: along_y(): return [jnp.stack([column[n] for column in columns]) for n in range(INNER)]]
    all_to_all x1, blocking collectives: 24.6 us -> 20.2 us  [shards(): lax.all_to_all(terms, 'fsdp', split_axis=0, concat_axis=0, tiled=True)]
    pallas_call x2 -> x4, Pallas kernels: 23.5 us -> 27.9 us  [the longest x2 21.2 us: head_terms(): pl.pallas_call(functools.partial(terms_kernel, head, len(rows)), out_shap...]
    concatenate x3 -> x4, other arithmetic: 0.02 us -> 3.35 us  [gather_shares(): shares = jnp.concatenate(parts, axis=0)]
  transfers between devices with their start and end apart: 7 -> 13, of which waited for: 4 -> 10; matrix products, arithmetic and copies ran while one was open for 1% -> 6% of each run, Pallas kernels for 0% -> 6%
where the time goes in v4:
time: 241 us; the launch traced here: 240 us
  waiting for transfers between devices  105 us (44%)
  starting transfers between devices  70.4 us (29%)
  Pallas kernels  27.9 us (12%)
  blocking collectives  20.2 us (8%)
  local copies, waits for them, and re-layouts  9.11 us (4%)
  other arithmetic  6.95 us (3%)
    ppermute x12, waiting for transfers between devices, permute(): return lax.ppermute(block, axis, pairs)  105 us
    ppermute x12, starting transfers between devices, permute(): return lax.ppermute(block, axis, pairs)  52 us
    pallas_call x2, Pallas kernels, head_terms(): pl.pallas_call(functools.partial(terms_kernel, head, len(rows)), out_shap...  21.2 us
    all_to_all x1, blocking collectives, shards(): lax.all_to_all(terms, 'fsdp', split_axis=0, concat_axis=0, tiled=True)  20.2 us
    all_to_all x1, starting transfers between devices, shards(): first = lax.all_to_all(first, 'sp', split_axis=0, concat_axis=0, tiled=True)  18.4 us
    pallas_call x2, Pallas kernels, pack(): pl.pallas_call(body, out_shape=jax.ShapeDtypeStruct((groups, rows, width)...  6.68 us
  transfers between devices with their start and end apart: 13, of which 10 were waited for; matrix products, arithmetic and copies ran while one was open for 6% of the time, Pallas kernels for 6%

profile of v4, /device:TPU:1, one launch (start us, length us, event | category | flops | bytes accessed | tf_op | source)
XLA Modules:
  0.0 240.4 jit_solution(7890115033970622441)
XLA Ops:
  0.6 3.3 %pack_head.2 = bf16[16,512,128]{2,1,0:T(8,128)(2,1)} custom-call(bf16[1,128,4096]{2,1,0:T(8,128)(2,1)} %refs_0_.2, bf16[1,128,4096]{2,1,0:T(8,128)(2,1)} %refs_1_.2, bf16[1,128,4096]{2,1,0:T(8,128)(2,1)} %refs_2_.2, bf16[1,128,4096]{2,1,0:T(8,128)(2,1)} %refs_3_.2), custom_call_target="tpu_custom_call" | custom-call | bytes 6291456 | tf_op jit(solution)/shard_map/pack_head/pallas_call | solution.py:58
  4.0 18.4 %all-to-all-start = ((bf16[16,512,128]{2,1,0:T(8,128)(2,1)}), bf16[16,512,128]{2,1,0:T(8,128)(2,1)S(1)}, u32[]{:S(2)}, u32[]{:S(2)}) async-start(bf16[16,512,128]{2,1,0:T(8,128)(2,1)} %pack_head.2), calls=%async_computation | async-start | bytes 4194304 | tf_op jit(solution)/shard_map/all_to_all | solution.py:272
  22.4 3.3 %pack_head.3 = bf16[16,512,128]{2,1,0:T(8,128)(2,1)} custom-call(bf16[1,128,4096]{2,1,0:T(8,128)(2,1)} %refs_0_.2, bf16[1,128,4096]{2,1,0:T(8,128)(2,1)} %refs_1_.2, bf16[1,128,4096]{2,1,0:T(8,128)(2,1)} %refs_2_.2, bf16[1,128,4096]{2,1,0:T(8,128)(2,1)} %refs_3_.2), custom_call_target="tpu_custom_call" | custom-call | bytes 6291456 | tf_op jit(solution)/shard_map/pack_head/pallas_call | solution.py:58
  25.7 2.6 %fusion.13 = (bf16[4,512,128]{2,1,0:T(8,128)(2,1)}, bf16[4,512,128]{2,1,0:T(8,128)(2,1)}, bf16[4,512,128]{2,1,0:T(8,128)(2,1)}) fusion(bf16[16,512,128]{2,1,0:T(8,128)(2,1)} %pack_head.3), kind=kLoop, calls=%fused_computation.39 | loop fusion | bytes 3145728 | tf_op jit(solution)/shard_map/slice | solution.py:297
  28.3 3.2 %collective-permute-start.3 = (bf16[4,512,128]{2,1,0:T(8,128)(2,1)}, bf16[4,512,128]{2,1,0:T(8,128)(2,1)}, u32[]{:S(2)}, u32[]{:S(2)}) collective-permute-start(bf16[4,512,128]{2,1,0:T(8,128)(2,1)} %get-tuple-element.34), channel_id=1, source_target_pairs={{0,4},{1,5},{2,6},{3,7},{4,0},{5,1},{6,2},{7,3},{8,12},{9,13},{10,... | collective-permute-start | bytes 1572872 | tf_op jit(solution)/shard_map/ppermute | solution.py:291
  31.6 4.3 %collective-permute-start.4 = (bf16[4,512,128]{2,1,0:T(8,128)(2,1)}, bf16[4,512,128]{2,1,0:T(8,128)(2,1)S(1)}, u32[]{:S(2)}, u32[]{:S(2)}) collective-permute-start(bf16[4,512,128]{2,1,0:T(8,128)(2,1)} %get-tuple-element.36), channel_id=1, source_target_pairs={{0,8},{1,9},{2,10},{3,11},{4,12},{5,13},{6,14},{7,15},{8,0},{9,1},... | collective-permute-start | bytes 1572872 | tf_op jit(solution)/shard_map/ppermute | solution.py:291
  35.9 2.0 collective-permute-start.5
  38.5 3.7 %collective-permute-start = (f32[1,2,2,4]{3,2,1,0:T(2,128)}, f32[1,2,2,4]{3,2,1,0:T(2,128)}, u32[]{:S(2)}, u32[]{:S(2)}) collective-permute-start(f32[1,2,2,4]{3,2,1,0:T(2,128)} %maximum_bitcast_fusion.1), channel_id=1, source_target_pairs={{0,16},{16,0},{32,48},{48,32},{64,80},{80,64},{96,112},{112,96},{1... | collective-permute-start | bytes 200 | tf_op jit(solution)/shard_map/ppermute | solution.py:291
  42.2 1.8 fusion.12
  44.8 1.3 pad_maximum_fusion.7
  46.0 3.1 %collective-permute-start.1 = (f32[2,2,2,4]{3,2,1,0:T(2,128)}, f32[2,2,2,4]{3,2,1,0:T(2,128)}, u32[]{:S(2)}, u32[]{:S(2)}) collective-permute-start(f32[2,2,2,4]{3,2,1,0:T(2,128)} %pad_maximum_fusion.7), channel_id=1, source_target_pairs={{0,128},{16,144},{32,160},{48,176},{64,192},{80,208},{96,224},{112... | collective-permute-start | bytes 392 | tf_op jit(solution)/shard_map/ppermute | solution.py:291
  49.2 1.8 collective-permute-done.1
  51.7 4.6 %collective-permute-start.2 = (f32[4,2,2,4]{3,2,1,0:T(2,128)S(1)}, f32[4,2,2,4]{3,2,1,0:T(2,128)S(1)}, u32[]{:S(2)}, u32[]{:S(2)}) collective-permute-start(f32[4,2,2,4]{3,2,1,0:T(2,128)S(1)} %pad_maximum_fusion.5), channel_id=1, source_target_pairs={{0,256},{16,272},{32,288},{48,304},{64,320},{80,336},{96,352},{112... | collective-permute-start | bytes 776 | tf_op jit(solution)/shard_map/ppermute | solution.py:291
  56.3 1.5 collective-permute-done.2
  57.9 1.3 pad_maximum_fusion.4
  60.3 7.8 %collective-permute-done.4 = bf16[4,512,128]{2,1,0:T(8,128)(2,1)S(1)} collective-permute-done((bf16[4,512,128]{2,1,0:T(8,128)(2,1)}, bf16[4,512,128]{2,1,0:T(8,128)(2,1)S(1)}, u32[]{:S(2)}, u32[]{:S(2)}) %collective-permute-start.4) | collective-permute-done | bytes 524320 | tf_op jit(solution)/shard_map/ppermute | solution.py:291
  68.1 2.1 collective-permute-done.5
  72.2 1.9 collective-permute-start.6
  74.3 4.0 %collective-permute-start.7 = (f32[8,2,2,4]{3,2,1,0:T(2,128)}, f32[8,2,2,4]{3,2,1,0:T(2,128)S(1)}, u32[]{:S(2)}, u32[]{:S(2)}) collective-permute-start(f32[8,2,2,4]{3,2,1,0:T(2,128)} %pad_maximum_fusion.4), channel_id=1, source_target_pairs={{0,64},{16,80},{32,96},{48,112},{64,0},{80,16},{96,32},{112,48},{1... | collective-permute-start | bytes 1544 | tf_op jit(solution)/shard_map/ppermute | solution.py:291
  78.4 3.3 %collective-permute-start.8 = (f32[8,2,2,4]{3,2,1,0:T(2,128)}, f32[8,2,2,4]{3,2,1,0:T(2,128)S(1)}, u32[]{:S(2)}, u32[]{:S(2)}) collective-permute-start(f32[8,2,2,4]{3,2,1,0:T(2,128)} %pad_maximum_fusion.4), channel_id=1, source_target_pairs={{0,96},{16,112},{32,64},{48,80},{64,32},{80,48},{96,0},{112,16},{1... | collective-permute-start | bytes 1544 | tf_op jit(solution)/shard_map/ppermute | solution.py:291
  82.5 12.1 %collective-permute-start.10 = (bf16[4,512,128]{2,1,0:T(8,128)(2,1)}, bf16[4,512,128]{2,1,0:T(8,128)(2,1)S(1)}, u32[]{:S(2)}, u32[]{:S(2)}) collective-permute-start(bf16[4,512,128]{2,1,0:T(8,128)(2,1)} %get-tuple-element.28), channel_id=1, source_target_pairs={{0,2},{1,3},{2,0},{3,1},{4,6},{5,7},{6,4},{7,5},{8,10},{9,11},{10,... | collective-permute-start | bytes 1572872 | tf_op jit(solution)/shard_map/ppermute | solution.py:291
  94.7 3.0 %collective-permute-start.11 = (bf16[4,512,128]{2,1,0:T(8,128)(2,1)}, bf16[4,512,128]{2,1,0:T(8,128)(2,1)}, u32[]{:S(2)}, u32[]{:S(2)}) collective-permute-start(bf16[4,512,128]{2,1,0:T(8,128)(2,1)} %get-tuple-element.29), channel_id=1, source_target_pairs={{0,3},{1,2},{2,1},{3,0},{4,7},{5,6},{6,5},{7,4},{8,11},{9,10},{10,... | collective-permute-start | bytes 1572872 | tf_op jit(solution)/shard_map/ppermute | solution.py:291
  97.6 10.1 %collective-permute-done.6 = f32[8,2,2,4]{3,2,1,0:T(2,128)S(1)} collective-permute-done((f32[8,2,2,4]{3,2,1,0:T(2,128)}, f32[8,2,2,4]{3,2,1,0:T(2,128)S(1)}, u32[]{:S(2)}, u32[]{:S(2)}) %collective-permute-start.6) | collective-permute-done | bytes 544 | tf_op jit(solution)/shard_map/ppermute | solution.py:291
  107.7 6.7 %collective-permute-start.9 = (bf16[4,512,128]{2,1,0:T(8,128)(2,1)}, bf16[4,512,128]{2,1,0:T(8,128)(2,1)}, u32[]{:S(2)}, u32[]{:S(2)}) collective-permute-start(bf16[4,512,128]{2,1,0:T(8,128)(2,1)} %get-tuple-element.27), channel_id=1, source_target_pairs={{0,1},{1,0},{2,3},{3,2},{4,5},{5,4},{6,7},{7,6},{8,9},{9,8},{10,11... | collective-permute-start | bytes 1572872 | tf_op jit(solution)/shard_map/ppermute | solution.py:291
  114.5 5.6 %collective-permute-done.7 = f32[8,2,2,4]{3,2,1,0:T(2,128)S(1)} collective-permute-done((f32[8,2,2,4]{3,2,1,0:T(2,128)}, f32[8,2,2,4]{3,2,1,0:T(2,128)S(1)}, u32[]{:S(2)}, u32[]{:S(2)}) %collective-permute-start.7) | collective-permute-done | bytes 544 | tf_op jit(solution)/shard_map/ppermute | solution.py:291
  120.2 44.4 %collective-permute-done.8 = f32[8,2,2,4]{3,2,1,0:T(2,128)S(1)} collective-permute-done((f32[8,2,2,4]{3,2,1,0:T(2,128)}, f32[8,2,2,4]{3,2,1,0:T(2,128)S(1)}, u32[]{:S(2)}, u32[]{:S(2)}) %collective-permute-start.8) | collective-permute-done | bytes 544 | tf_op jit(solution)/shard_map/ppermute | solution.py:291
  165.4 10.2 %head_terms.2 = f32[2,128]{1,0:T(2,128)S(1)} custom-call(s32[16,6]{1,0:T(8,128)S(1)} %copy.40.win_ref, s32[2048]{0:T(1024)S(1)} %get-tuple-element.51.starts_ref, bf16[16,512,128]{2,1,0:T(8,128)(2,1)S(1)} %all-to-all-done.refs_0_, f32[2,128]{1,0:T(2,128)S(1)} %squeeze.14.refs_1_.refs_4_, f32[2,128]{1,0:T(2,128)S(1)} %squeeze.15.refs_2_.refs_5_), custom_call_target="tpu_custom_call" | custom-call | flops 2013265920 | bytes 2097152 | tf_op jit(solution)/shard_map/head_terms/pallas_call | solution.py:233
  175.6 1.7 collective-permute-done.10.refs_2_
  177.3 9.4 %collective-permute-done.11.refs_3_ = bf16[4,512,128]{2,1,0:T(8,128)(2,1)} collective-permute-done((bf16[4,512,128]{2,1,0:T(8,128)(2,1)}, bf16[4,512,128]{2,1,0:T(8,128)(2,1)}, u32[]{:S(2)}, u32[]{:S(2)}) %collective-permute-start.11) | collective-permute-done | bytes 524320 | tf_op jit(solution)/shard_map/ppermute | solution.py:291
  186.8 20.5 %collective-permute-done.9.refs_1_ = bf16[4,512,128]{2,1,0:T(8,128)(2,1)} collective-permute-done((bf16[4,512,128]{2,1,0:T(8,128)(2,1)}, bf16[4,512,128]{2,1,0:T(8,128)(2,1)}, u32[]{:S(2)}, u32[]{:S(2)}) %collective-permute-start.9) | collective-permute-done | bytes 524320 | tf_op jit(solution)/shard_map/ppermute | solution.py:291
  207.3 11.0 %head_terms.3 = f32[2,128]{1,0:T(2,128)S(1)} custom-call(s32[16,6]{1,0:T(8,128)S(1)} %copy.40.win_ref, s32[2048]{0:T(1024)S(1)} %get-tuple-element.25.starts_ref, bf16[4,512,128]{2,1,0:T(8,128)(2,1)S(1)} %get-tuple-element.26.refs_0_, bf16[4,512,128]{2,1,0:T(8,128)(2,1)} %collective-permute-done.9.refs_1_, ...), custom_call_target="tpu_custom_call" | custom-call | flops 2013265920 | bytes 2097152 | tf_op jit(solution)/shard_map/head_terms/pallas_call | solution.py:233
  218.8 20.2 %all_to_all.14 = f32[32,1,16]{2,1,0:T(1,128)S(1)} all-to-all(f32[32,1,16]{2,1,0:T(1,128)S(1)} %copy.45), channel_id=1, replica_groups=mesh['fsdp'=32,'sp'=16] {'fsdp'}, dimensions={0} | all-to-all | bytes 4096 | tf_op jit(solution)/shard_map/all_to_all | solution.py:284
  (47 shorter events, 9.1 us)
Async XLA Ops:
  4.0 161.4 %all-to-all-start = ((bf16[16,512,128]{2,1,0:T(8,128)(2,1)}), bf16[16,512,128]{2,1,0:T(8,128)(2,1)S(1)}, u32[]{:S(2)}, u32[]{:S(2)}) async-start(bf16[16,512,128]{2,1,0:T(8,128)(2,1)} %pack_head.2), calls=%async_computation | async-start | bytes 4194304 | tf_op jit(solution)/shard_map/all_to_all | solution.py:272
  25.7 12.2 %copy-start.2 = (f32[2,4]{1,0:T(2,128)S(1)}, f32[2,4]{1,0:T(2,128)}, u32[]{:S(2)}) copy-start(f32[2,4]{1,0:T(2,128)} %param.14) | copy-start | bytes 100
  25.7 12.2 %copy-start.3 = (f32[2,4]{1,0:T(2,128)S(1)}, f32[2,4]{1,0:T(2,128)}, u32[]{:S(2)}) copy-start(f32[2,4]{1,0:T(2,128)} %param.13) | copy-start | bytes 100
  28.3 30.8 %collective-permute-start.3 = (bf16[4,512,128]{2,1,0:T(8,128)(2,1)}, bf16[4,512,128]{2,1,0:T(8,128)(2,1)}, u32[]{:S(2)}, u32[]{:S(2)}) collective-permute-start(bf16[4,512,128]{2,1,0:T(8,128)(2,1)} %get-tuple-element.34), channel_id=1, source_target_pairs={{0,4},{1,5},{2,6},{3,7},{4,0},{5,1},{6,2},{7,3},{8,12},{9,13},{10,... | collective-permute-start | bytes 1572872 | tf_op jit(solution)/shard_map/ppermute | solution.py:291
  31.6 36.5 %collective-permute-start.4 = (bf16[4,512,128]{2,1,0:T(8,128)(2,1)}, bf16[4,512,128]{2,1,0:T(8,128)(2,1)S(1)}, u32[]{:S(2)}, u32[]{:S(2)}) collective-permute-start(bf16[4,512,128]{2,1,0:T(8,128)(2,1)} %get-tuple-element.36), channel_id=1, source_target_pairs={{0,8},{1,9},{2,10},{3,11},{4,12},{5,13},{6,14},{7,15},{8,0},{9,1},... | collective-permute-start | bytes 1572872 | tf_op jit(solution)/shard_map/ppermute | solution.py:291
  35.9 34.3 %collective-permute-start.5 = (bf16[4,512,128]{2,1,0:T(8,128)(2,1)}, bf16[4,512,128]{2,1,0:T(8,128)(2,1)S(1)}, u32[]{:S(2)}, u32[]{:S(2)}) collective-permute-start(bf16[4,512,128]{2,1,0:T(8,128)(2,1)} %get-tuple-element.35), channel_id=1, source_target_pairs={{0,12},{1,13},{2,14},{3,15},{4,8},{5,9},{6,10},{7,11},{8,4},{9,5},... | collective-permute-start | bytes 1572872 | tf_op jit(solution)/shard_map/ppermute | solution.py:291
  38.5 6.2 %collective-permute-start = (f32[1,2,2,4]{3,2,1,0:T(2,128)}, f32[1,2,2,4]{3,2,1,0:T(2,128)}, u32[]{:S(2)}, u32[]{:S(2)}) collective-permute-start(f32[1,2,2,4]{3,2,1,0:T(2,128)} %maximum_bitcast_fusion.1), channel_id=1, source_target_pairs={{0,16},{16,0},{32,48},{48,32},{64,80},{80,64},{96,112},{112,96},{1... | collective-permute-start | bytes 200 | tf_op jit(solution)/shard_map/ppermute | solution.py:291
  46.0 5.0 %collective-permute-start.1 = (f32[2,2,2,4]{3,2,1,0:T(2,128)}, f32[2,2,2,4]{3,2,1,0:T(2,128)}, u32[]{:S(2)}, u32[]{:S(2)}) collective-permute-start(f32[2,2,2,4]{3,2,1,0:T(2,128)} %pad_maximum_fusion.7), channel_id=1, source_target_pairs={{0,128},{16,144},{32,160},{48,176},{64,192},{80,208},{96,224},{112... | collective-permute-start | bytes 392 | tf_op jit(solution)/shard_map/ppermute | solution.py:291
  49.2 21.1 %copy-start = (bf16[1,512,128]{2,1,0:T(8,128)(2,1)S(1)}, bf16[1,512,128]{2,1,0:T(8,128)(2,1)}, u32[]{:S(2)}) copy-start(bf16[1,512,128]{2,1,0:T(8,128)(2,1)} %get-tuple-element.31) | copy-start | bytes 393220
  51.7 6.2 %collective-permute-start.2 = (f32[4,2,2,4]{3,2,1,0:T(2,128)S(1)}, f32[4,2,2,4]{3,2,1,0:T(2,128)S(1)}, u32[]{:S(2)}, u32[]{:S(2)}) collective-permute-start(f32[4,2,2,4]{3,2,1,0:T(2,128)S(1)} %pad_maximum_fusion.5), channel_id=1, source_target_pairs={{0,256},{16,272},{32,288},{48,304},{64,320},{80,336},{96,352},{112... | collective-permute-start | bytes 776 | tf_op jit(solution)/shard_map/ppermute | solution.py:291
  70.2 3.9 %copy-start.4 = (s32[32]{0:T(128)S(1)}, s32[32]{0:T(128)}, u32[]{:S(2)}) copy-start(s32[32]{0:T(128)} %constant.63.clone) | copy-start | bytes 388
  71.3 2.9 %copy-start.1 = (s32[16,6]{0,1:T(8,128)S(1)}, s32[16,6]{0,1:T(8,128)}, u32[]{:S(2)}) copy-start(s32[16,6]{0,1:T(8,128)} %param.15) | copy-start | bytes 1156
  72.2 35.5 %collective-permute-start.6 = (f32[8,2,2,4]{3,2,1,0:T(2,128)}, f32[8,2,2,4]{3,2,1,0:T(2,128)S(1)}, u32[]{:S(2)}, u32[]{:S(2)}) collective-permute-start(f32[8,2,2,4]{3,2,1,0:T(2,128)} %pad_maximum_fusion.4), channel_id=1, source_target_pairs={{0,32},{16,48},{32,0},{48,16},{64,96},{80,112},{96,64},{112,80},{1... | collective-permute-start | bytes 1544 | tf_op jit(solution)/shard_map/ppermute | solution.py:291
  74.3 45.7 %collective-permute-start.7 = (f32[8,2,2,4]{3,2,1,0:T(2,128)}, f32[8,2,2,4]{3,2,1,0:T(2,128)S(1)}, u32[]{:S(2)}, u32[]{:S(2)}) collective-permute-start(f32[8,2,2,4]{3,2,1,0:T(2,128)} %pad_maximum_fusion.4), channel_id=1, source_target_pairs={{0,64},{16,80},{32,96},{48,112},{64,0},{80,16},{96,32},{112,48},{1... | collective-permute-start | bytes 1544 | tf_op jit(solution)/shard_map/ppermute | solution.py:291
  78.4 86.2 %collective-permute-start.8 = (f32[8,2,2,4]{3,2,1,0:T(2,128)}, f32[8,2,2,4]{3,2,1,0:T(2,128)S(1)}, u32[]{:S(2)}, u32[]{:S(2)}) collective-permute-start(f32[8,2,2,4]{3,2,1,0:T(2,128)} %pad_maximum_fusion.4), channel_id=1, source_target_pairs={{0,96},{16,112},{32,64},{48,80},{64,32},{80,48},{96,0},{112,16},{1... | collective-permute-start | bytes 1544 | tf_op jit(solution)/shard_map/ppermute | solution.py:291
  82.5 94.8 %collective-permute-start.10 = (bf16[4,512,128]{2,1,0:T(8,128)(2,1)}, bf16[4,512,128]{2,1,0:T(8,128)(2,1)S(1)}, u32[]{:S(2)}, u32[]{:S(2)}) collective-permute-start(bf16[4,512,128]{2,1,0:T(8,128)(2,1)} %get-tuple-element.28), channel_id=1, source_target_pairs={{0,2},{1,3},{2,0},{3,1},{4,6},{5,7},{6,4},{7,5},{8,10},{9,11},{10,... | collective-permute-start | bytes 1572872 | tf_op jit(solution)/shard_map/ppermute | solution.py:291
  94.7 92.1 %collective-permute-start.11 = (bf16[4,512,128]{2,1,0:T(8,128)(2,1)}, bf16[4,512,128]{2,1,0:T(8,128)(2,1)}, u32[]{:S(2)}, u32[]{:S(2)}) collective-permute-start(bf16[4,512,128]{2,1,0:T(8,128)(2,1)} %get-tuple-element.29), channel_id=1, source_target_pairs={{0,3},{1,2},{2,1},{3,0},{4,7},{5,6},{6,5},{7,4},{8,11},{9,10},{10,... | collective-permute-start | bytes 1572872 | tf_op jit(solution)/shard_map/ppermute | solution.py:291
  107.7 99.6 %collective-permute-start.9 = (bf16[4,512,128]{2,1,0:T(8,128)(2,1)}, bf16[4,512,128]{2,1,0:T(8,128)(2,1)}, u32[]{:S(2)}, u32[]{:S(2)}) collective-permute-start(bf16[4,512,128]{2,1,0:T(8,128)(2,1)} %get-tuple-element.27), channel_id=1, source_target_pairs={{0,1},{1,0},{2,3},{3,2},{4,5},{5,4},{6,7},{7,6},{8,9},{9,8},{10,11... | collective-permute-start | bytes 1572872 | tf_op jit(solution)/shard_map/ppermute | solution.py:291

commit v5 on v4

--- a/solution.py
+++ b/solution.py
@@ -144,7 +144,7 @@
         return carry
 
     gather(0, even_ref)
-    lax.fori_loop(0, tiles // 2, in_order, 0, unroll=2)
+    lax.fori_loop(0, tiles // 2, in_order, 0, unroll=8)
     blank = jnp.zeros((TILE, width), jnp.bfloat16)
     spans = [slice(n * TILE, (n + 1) * TILE) for n in range(count)]
 
@@ -215,7 +215,7 @@
             query_terms(1 - slot, jnp.maximum(tile - 1, 0))
         return carry
 
-    lax.fori_loop(0, tiles // 2, attend, 0, unroll=2)
+    lax.fori_loop(0, tiles // 2, attend, 0, unroll=8)
     query_terms(1, tiles - 1)
     out_ref[0:1, :] = jnp.sum(acc_ref[0], axis=0, keepdims=True) * scale
     out_ref[1:2, :] = jnp.sum(acc_ref[1], axis=0, keepdims=True) * scale / gain_k
@@ -274,6 +274,7 @@
     second = along_y(pack(arrays, 1, groups, heads, width, "sp"))
     shares, *second = lax.optimization_barrier((shares, *second))
     shares, offsets = gather_shares(shares, offsets, ((2, 4, 6),))
+    shares, second[2] = lax.optimization_barrier((shares, second[2]))
     gains = in_channel_order(shares, jnp.array(offsets, jnp.int32), spread)
     second, starts = along_z(second, order, tokens)
     terms = [head_terms([first], order * PARTS, gains[0], gains[1], windows, 0)]

time: 241 us -> 241 us (level)
  blocking collectives: 20.2 us -> 24.9 us
  waiting for transfers between devices: 105 us -> 102 us
  Pallas kernels: 27.9 us -> 25.1 us
    all_to_all x1, blocking collectives: 20.2 us -> 24.9 us  [shards(): lax.all_to_all(terms, 'fsdp', split_axis=0, concat_axis=0, tiled=True)]
    ppermute x12, waiting for transfers between devices: 105 us -> 102 us  [permute(): return lax.ppermute(block, axis, pairs)]
    pallas_call x2, Pallas kernels: 21.2 us -> 18.4 us  [head_terms(): pl.pallas_call(functools.partial(terms_kernel, head, len(rows)), out_shap...]
  transfers between devices with their start and end apart: 13 -> 13, of which waited for: 10 -> 8; matrix products, arithmetic and copies ran while one was open for 6% -> 6% of each run, Pallas kernels for 6% -> 5%
where the time goes in v5:
time: 241 us; the launch traced here: 240 us
  waiting for transfers between devices  102 us (42%)
  starting transfers between devices  71.5 us (30%)
  Pallas kernels  25.1 us (10%)
  blocking collectives  24.9 us (10%)
  local copies, waits for them, and re-layouts  9.06 us (4%)
  other arithmetic  6.97 us (3%)
    ppermute x12, waiting for transfers between devices, permute(): return lax.ppermute(block, axis, pairs)  102 us
    ppermute x12, starting transfers between devices, permute(): return lax.ppermute(block, axis, pairs)  53.1 us
    all_to_all x1, blocking collectives, shards(): lax.all_to_all(terms, 'fsdp', split_axis=0, concat_axis=0, tiled=True)  24.9 us
    pallas_call x2, Pallas kernels, head_terms(): pl.pallas_call(functools.partial(terms_kernel, head, len(rows)), out_shap...  18.4 us
    all_to_all x1, starting transfers between devices, shards(): first = lax.all_to_all(first, 'sp', split_axis=0, concat_axis=0, tiled=True)  18.4 us
    pallas_call x2, Pallas kernels, pack(): pl.pallas_call(body, out_shape=jax.ShapeDtypeStruct((groups, rows, width)...  6.69 us
  transfers between devices with their start and end apart: 13, of which 8 were waited for; matrix products, arithmetic and copies ran while one was open for 6% of the time, Pallas kernels for 5%

profile of v5, /device:TPU:1, one launch (start us, length us, event | category | flops | bytes accessed | tf_op | source)
XLA Modules:
  0.0 240.4 jit_solution(4945925902753853333)
XLA Ops:
  0.6 3.3 %pack_head.2 = bf16[16,512,128]{2,1,0:T(8,128)(2,1)} custom-call(bf16[1,128,4096]{2,1,0:T(8,128)(2,1)} %refs_0_.2, bf16[1,128,4096]{2,1,0:T(8,128)(2,1)} %refs_1_.2, bf16[1,128,4096]{2,1,0:T(8,128)(2,1)} %refs_2_.2, bf16[1,128,4096]{2,1,0:T(8,128)(2,1)} %refs_3_.2), custom_call_target="tpu_custom_call" | custom-call | bytes 6291456 | tf_op jit(solution)/shard_map/pack_head/pallas_call | solution.py:58
  4.0 18.4 %all-to-all-start = ((bf16[16,512,128]{2,1,0:T(8,128)(2,1)}), bf16[16,512,128]{2,1,0:T(8,128)(2,1)S(1)}, u32[]{:S(2)}, u32[]{:S(2)}) async-start(bf16[16,512,128]{2,1,0:T(8,128)(2,1)} %pack_head.2), calls=%async_computation | async-start | bytes 4194304 | tf_op jit(solution)/shard_map/all_to_all | solution.py:272
  22.4 3.3 %pack_head.3 = bf16[16,512,128]{2,1,0:T(8,128)(2,1)} custom-call(bf16[1,128,4096]{2,1,0:T(8,128)(2,1)} %refs_0_.2, bf16[1,128,4096]{2,1,0:T(8,128)(2,1)} %refs_1_.2, bf16[1,128,4096]{2,1,0:T(8,128)(2,1)} %refs_2_.2, bf16[1,128,4096]{2,1,0:T(8,128)(2,1)} %refs_3_.2), custom_call_target="tpu_custom_call" | custom-call | bytes 6291456 | tf_op jit(solution)/shard_map/pack_head/pallas_call | solution.py:58
  25.8 2.5 %fusion.13 = (bf16[4,512,128]{2,1,0:T(8,128)(2,1)}, bf16[4,512,128]{2,1,0:T(8,128)(2,1)}, bf16[4,512,128]{2,1,0:T(8,128)(2,1)}) fusion(bf16[16,512,128]{2,1,0:T(8,128)(2,1)} %pack_head.3), kind=kLoop, calls=%fused_computation.39 | loop fusion | bytes 3145728 | tf_op jit(solution)/shard_map/slice | solution.py:298
  28.3 3.3 %collective-permute-start.3 = (bf16[4,512,128]{2,1,0:T(8,128)(2,1)}, bf16[4,512,128]{2,1,0:T(8,128)(2,1)}, u32[]{:S(2)}, u32[]{:S(2)}) collective-permute-start(bf16[4,512,128]{2,1,0:T(8,128)(2,1)} %get-tuple-element.38), channel_id=1, source_target_pairs={{0,4},{1,5},{2,6},{3,7},{4,0},{5,1},{6,2},{7,3},{8,12},{9,13},{10,... | collective-permute-start | bytes 1572872 | tf_op jit(solution)/shard_map/ppermute | solution.py:292
  31.6 4.3 %collective-permute-start.4 = (bf16[4,512,128]{2,1,0:T(8,128)(2,1)}, bf16[4,512,128]{2,1,0:T(8,128)(2,1)S(1)}, u32[]{:S(2)}, u32[]{:S(2)}) collective-permute-start(bf16[4,512,128]{2,1,0:T(8,128)(2,1)} %get-tuple-element.40), channel_id=1, source_target_pairs={{0,8},{1,9},{2,10},{3,11},{4,12},{5,13},{6,14},{7,15},{8,0},{9,1},... | collective-permute-start | bytes 1572872 | tf_op jit(solution)/shard_map/ppermute | solution.py:292
  35.9 2.0 collective-permute-start.5
  38.5 3.7 %collective-permute-start = (f32[1,2,2,4]{3,2,1,0:T(2,128)}, f32[1,2,2,4]{3,2,1,0:T(2,128)}, u32[]{:S(2)}, u32[]{:S(2)}) collective-permute-start(f32[1,2,2,4]{3,2,1,0:T(2,128)} %maximum_bitcast_fusion.1), channel_id=1, source_target_pairs={{0,16},{16,0},{32,48},{48,32},{64,80},{80,64},{96,112},{112,96},{1... | collective-permute-start | bytes 200 | tf_op jit(solution)/shard_map/ppermute | solution.py:292
  42.2 1.8 fusion.12
  44.7 1.3 pad_maximum_fusion.7
  46.0 3.1 %collective-permute-start.1 = (f32[2,2,2,4]{3,2,1,0:T(2,128)}, f32[2,2,2,4]{3,2,1,0:T(2,128)}, u32[]{:S(2)}, u32[]{:S(2)}) collective-permute-start(f32[2,2,2,4]{3,2,1,0:T(2,128)} %pad_maximum_fusion.7), channel_id=1, source_target_pairs={{0,128},{16,144},{32,160},{48,176},{64,192},{80,208},{96,224},{112... | collective-permute-start | bytes 392 | tf_op jit(solution)/shard_map/ppermute | solution.py:292
  49.1 1.8 collective-permute-done.1
  51.7 4.6 %collective-permute-start.2 = (f32[4,2,2,4]{3,2,1,0:T(2,128)S(1)}, f32[4,2,2,4]{3,2,1,0:T(2,128)S(1)}, u32[]{:S(2)}, u32[]{:S(2)}) collective-permute-start(f32[4,2,2,4]{3,2,1,0:T(2,128)S(1)} %pad_maximum_fusion.5), channel_id=1, source_target_pairs={{0,256},{16,272},{32,288},{48,304},{64,320},{80,336},{96,352},{112... | collective-permute-start | bytes 776 | tf_op jit(solution)/shard_map/ppermute | solution.py:292
  56.3 1.5 collective-permute-done.2
  57.8 1.3 pad_maximum_fusion.4
  59.1 1.1 fusion.14
  60.3 7.7 %collective-permute-done.4 = bf16[4,512,128]{2,1,0:T(8,128)(2,1)S(1)} collective-permute-done((bf16[4,512,128]{2,1,0:T(8,128)(2,1)}, bf16[4,512,128]{2,1,0:T(8,128)(2,1)S(1)}, u32[]{:S(2)}, u32[]{:S(2)}) %collective-permute-start.4) | collective-permute-done | bytes 524320 | tf_op jit(solution)/shard_map/ppermute | solution.py:292
  68.1 2.1 collective-permute-done.5
  70.2 1.1 pad_maximum_fusion.2
  72.3 1.9 collective-permute-start.6
  74.3 4.0 %collective-permute-start.7 = (f32[8,2,2,4]{3,2,1,0:T(2,128)}, f32[8,2,2,4]{3,2,1,0:T(2,128)S(1)}, u32[]{:S(2)}, u32[]{:S(2)}) collective-permute-start(f32[8,2,2,4]{3,2,1,0:T(2,128)} %pad_maximum_fusion.4), channel_id=1, source_target_pairs={{0,64},{16,80},{32,96},{48,112},{64,0},{80,16},{96,32},{112,48},{1... | collective-permute-start | bytes 1544 | tf_op jit(solution)/shard_map/ppermute | solution.py:292
  78.3 3.3 %collective-permute-start.8 = (f32[8,2,2,4]{3,2,1,0:T(2,128)}, f32[8,2,2,4]{3,2,1,0:T(2,128)S(1)}, u32[]{:S(2)}, u32[]{:S(2)}) collective-permute-start(f32[8,2,2,4]{3,2,1,0:T(2,128)} %pad_maximum_fusion.4), channel_id=1, source_target_pairs={{0,96},{16,112},{32,64},{48,80},{64,32},{80,48},{96,0},{112,16},{1... | collective-permute-start | bytes 1544 | tf_op jit(solution)/shard_map/ppermute | solution.py:292
  82.5 7.8 %collective-permute-start.11 = (bf16[4,512,128]{2,1,0:T(8,128)(2,1)}, bf16[4,512,128]{2,1,0:T(8,128)(2,1)S(1)}, u32[]{:S(2)}, u32[]{:S(2)}) collective-permute-start(bf16[4,512,128]{2,1,0:T(8,128)(2,1)} %get-tuple-element.33), channel_id=1, source_target_pairs={{0,3},{1,2},{2,1},{3,0},{4,7},{5,6},{6,5},{7,4},{8,11},{9,10},{10,... | collective-permute-start | bytes 1572872 | tf_op jit(solution)/shard_map/ppermute | solution.py:292
  90.3 6.5 %collective-permute-start.9 = (bf16[4,512,128]{2,1,0:T(8,128)(2,1)}, bf16[4,512,128]{2,1,0:T(8,128)(2,1)}, u32[]{:S(2)}, u32[]{:S(2)}) collective-permute-start(bf16[4,512,128]{2,1,0:T(8,128)(2,1)} %get-tuple-element.31), channel_id=1, source_target_pairs={{0,1},{1,0},{2,3},{3,2},{4,5},{5,4},{6,7},{7,6},{8,9},{9,8},{10,11... | collective-permute-start | bytes 1572872 | tf_op jit(solution)/shard_map/ppermute | solution.py:292
  96.9 10.8 %collective-permute-done.6 = f32[8,2,2,4]{3,2,1,0:T(2,128)S(1)} collective-permute-done((f32[8,2,2,4]{3,2,1,0:T(2,128)}, f32[8,2,2,4]{3,2,1,0:T(2,128)S(1)}, u32[]{:S(2)}, u32[]{:S(2)}) %collective-permute-start.6) | collective-permute-done | bytes 544 | tf_op jit(solution)/shard_map/ppermute | solution.py:292
  107.8 17.8 %collective-permute-done.7 = f32[8,2,2,4]{3,2,1,0:T(2,128)S(1)} collective-permute-done((f32[8,2,2,4]{3,2,1,0:T(2,128)}, f32[8,2,2,4]{3,2,1,0:T(2,128)S(1)}, u32[]{:S(2)}, u32[]{:S(2)}) %collective-permute-start.7) | collective-permute-done | bytes 544 | tf_op jit(solution)/shard_map/ppermute | solution.py:292
  125.6 17.8 %collective-permute-done.8 = f32[8,2,2,4]{3,2,1,0:T(2,128)S(1)} collective-permute-done((f32[8,2,2,4]{3,2,1,0:T(2,128)}, f32[8,2,2,4]{3,2,1,0:T(2,128)S(1)}, u32[]{:S(2)}, u32[]{:S(2)}) %collective-permute-start.8) | collective-permute-done | bytes 544 | tf_op jit(solution)/shard_map/ppermute | solution.py:292
  143.6 8.5 %collective-permute-start.10 = (bf16[4,512,128]{2,1,0:T(8,128)(2,1)}, bf16[4,512,128]{2,1,0:T(8,128)(2,1)}, u32[]{:S(2)}, u32[]{:S(2)}) collective-permute-start(bf16[4,512,128]{2,1,0:T(8,128)(2,1)} %get-tuple-element.32), channel_id=1, source_target_pairs={{0,2},{1,3},{2,0},{3,1},{4,6},{5,7},{6,4},{7,5},{8,10},{9,11},{10,... | collective-permute-start | bytes 1572872 | tf_op jit(solution)/shard_map/ppermute | solution.py:292
  152.7 8.8 %head_terms.2 = f32[2,128]{1,0:T(2,128)S(1)} custom-call(s32[16,6]{1,0:T(8,128)S(1)} %copy.40.win_ref, s32[2048]{0:T(1024)S(1)} %get-tuple-element.55.starts_ref, bf16[16,512,128]{2,1,0:T(8,128)(2,1)S(1)} %all-to-all-done.refs_0_, f32[2,128]{1,0:T(2,128)S(1)} %squeeze.14.refs_1_.refs_4_, f32[2,128]{1,0:T(2,128)S(1)} %squeeze.15.refs_2_.refs_5_), custom_call_target="tpu_custom_call" | custom-call | flops 2013265920 | bytes 2097152 | tf_op jit(solution)/shard_map/head_terms/pallas_call | solution.py:233
  161.5 42.5 %collective-permute-done.10.refs_2_ = bf16[4,512,128]{2,1,0:T(8,128)(2,1)} collective-permute-done((bf16[4,512,128]{2,1,0:T(8,128)(2,1)}, bf16[4,512,128]{2,1,0:T(8,128)(2,1)}, u32[]{:S(2)}, u32[]{:S(2)}) %collective-permute-start.10) | collective-permute-done | bytes 524320 | tf_op jit(solution)/shard_map/ppermute | solution.py:292
  204.0 9.6 %head_terms.3 = f32[2,128]{1,0:T(2,128)S(1)} custom-call(s32[16,6]{1,0:T(8,128)S(1)} %copy.40.win_ref, s32[2048]{0:T(1024)S(1)} %get-tuple-element.29.starts_ref, bf16[4,512,128]{2,1,0:T(8,128)(2,1)S(1)} %get-tuple-element.30.refs_0_, bf16[4,512,128]{2,1,0:T(8,128)(2,1)} %collective-permute-done.9.refs_1_, ...), custom_call_target="tpu_custom_call" | custom-call | flops 2013265920 | bytes 2097152 | tf_op jit(solution)/shard_map/head_terms/pallas_call | solution.py:233
  214.1 24.9 %all_to_all.14 = f32[32,1,16]{2,1,0:T(1,128)S(1)} all-to-all(f32[32,1,16]{2,1,0:T(1,128)S(1)} %copy.45), channel_id=1, replica_groups=mesh['fsdp'=32,'sp'=16] {'fsdp'}, dimensions={0} | all-to-all | bytes 4096 | tf_op jit(solution)/shard_map/all_to_all | solution.py:285
  (47 shorter events, 6.9 us)
Async XLA Ops:
  4.0 148.7 %all-to-all-start = ((bf16[16,512,128]{2,1,0:T(8,128)(2,1)}), bf16[16,512,128]{2,1,0:T(8,128)(2,1)S(1)}, u32[]{:S(2)}, u32[]{:S(2)}) async-start(bf16[16,512,128]{2,1,0:T(8,128)(2,1)} %pack_head.2), calls=%async_computation | async-start | bytes 4194304 | tf_op jit(solution)/shard_map/all_to_all | solution.py:272
  25.7 12.2 %copy-start.2 = (f32[2,4]{1,0:T(2,128)S(1)}, f32[2,4]{1,0:T(2,128)}, u32[]{:S(2)}) copy-start(f32[2,4]{1,0:T(2,128)} %param.14) | copy-start | bytes 100
  25.7 12.2 %copy-start.3 = (f32[2,4]{1,0:T(2,128)S(1)}, f32[2,4]{1,0:T(2,128)}, u32[]{:S(2)}) copy-start(f32[2,4]{1,0:T(2,128)} %param.13) | copy-start | bytes 100
  28.3 30.8 %collective-permute-start.3 = (bf16[4,512,128]{2,1,0:T(8,128)(2,1)}, bf16[4,512,128]{2,1,0:T(8,128)(2,1)}, u32[]{:S(2)}, u32[]{:S(2)}) collective-permute-start(bf16[4,512,128]{2,1,0:T(8,128)(2,1)} %get-tuple-element.38), channel_id=1, source_target_pairs={{0,4},{1,5},{2,6},{3,7},{4,0},{5,1},{6,2},{7,3},{8,12},{9,13},{10,... | collective-permute-start | bytes 1572872 | tf_op jit(solution)/shard_map/ppermute | solution.py:292
  31.6 36.5 %collective-permute-start.4 = (bf16[4,512,128]{2,1,0:T(8,128)(2,1)}, bf16[4,512,128]{2,1,0:T(8,128)(2,1)S(1)}, u32[]{:S(2)}, u32[]{:S(2)}) collective-permute-start(bf16[4,512,128]{2,1,0:T(8,128)(2,1)} %get-tuple-element.40), channel_id=1, source_target_pairs={{0,8},{1,9},{2,10},{3,11},{4,12},{5,13},{6,14},{7,15},{8,0},{9,1},... | collective-permute-start | bytes 1572872 | tf_op jit(solution)/shard_map/ppermute | solution.py:292
  35.9 34.3 %collective-permute-start.5 = (bf16[4,512,128]{2,1,0:T(8,128)(2,1)}, bf16[4,512,128]{2,1,0:T(8,128)(2,1)S(1)}, u32[]{:S(2)}, u32[]{:S(2)}) collective-permute-start(bf16[4,512,128]{2,1,0:T(8,128)(2,1)} %get-tuple-element.39), channel_id=1, source_target_pairs={{0,12},{1,13},{2,14},{3,15},{4,8},{5,9},{6,10},{7,11},{8,4},{9,5},... | collective-permute-start | bytes 1572872 | tf_op jit(solution)/shard_map/ppermute | solution.py:292
  38.5 6.2 %collective-permute-start = (f32[1,2,2,4]{3,2,1,0:T(2,128)}, f32[1,2,2,4]{3,2,1,0:T(2,128)}, u32[]{:S(2)}, u32[]{:S(2)}) collective-permute-start(f32[1,2,2,4]{3,2,1,0:T(2,128)} %maximum_bitcast_fusion.1), channel_id=1, source_target_pairs={{0,16},{16,0},{32,48},{48,32},{64,80},{80,64},{96,112},{112,96},{1... | collective-permute-start | bytes 200 | tf_op jit(solution)/shard_map/ppermute | solution.py:292
  46.0 5.0 %collective-permute-start.1 = (f32[2,2,2,4]{3,2,1,0:T(2,128)}, f32[2,2,2,4]{3,2,1,0:T(2,128)}, u32[]{:S(2)}, u32[]{:S(2)}) collective-permute-start(f32[2,2,2,4]{3,2,1,0:T(2,128)} %pad_maximum_fusion.7), channel_id=1, source_target_pairs={{0,128},{16,144},{32,160},{48,176},{64,192},{80,208},{96,224},{112... | collective-permute-start | bytes 392 | tf_op jit(solution)/shard_map/ppermute | solution.py:292
  49.1 21.1 %copy-start = (bf16[1,512,128]{2,1,0:T(8,128)(2,1)S(1)}, bf16[1,512,128]{2,1,0:T(8,128)(2,1)}, u32[]{:S(2)}) copy-start(bf16[1,512,128]{2,1,0:T(8,128)(2,1)} %get-tuple-element.35) | copy-start | bytes 393220
  51.7 6.2 %collective-permute-start.2 = (f32[4,2,2,4]{3,2,1,0:T(2,128)S(1)}, f32[4,2,2,4]{3,2,1,0:T(2,128)S(1)}, u32[]{:S(2)}, u32[]{:S(2)}) collective-permute-start(f32[4,2,2,4]{3,2,1,0:T(2,128)S(1)} %pad_maximum_fusion.5), channel_id=1, source_target_pairs={{0,256},{16,272},{32,288},{48,304},{64,320},{80,336},{96,352},{112... | collective-permute-start | bytes 776 | tf_op jit(solution)/shard_map/ppermute | solution.py:292
  70.2 4.0 %copy-start.4 = (s32[32]{0:T(128)S(1)}, s32[32]{0:T(128)}, u32[]{:S(2)}) copy-start(s32[32]{0:T(128)} %constant.63.clone) | copy-start | bytes 388
  71.3 10.3 %copy-start.1 = (s32[16,6]{0,1:T(8,128)S(1)}, s32[16,6]{0,1:T(8,128)}, u32[]{:S(2)}) copy-start(s32[16,6]{0,1:T(8,128)} %param.15) | copy-start | bytes 1156
  72.3 35.4 %collective-permute-start.6 = (f32[8,2,2,4]{3,2,1,0:T(2,128)}, f32[8,2,2,4]{3,2,1,0:T(2,128)S(1)}, u32[]{:S(2)}, u32[]{:S(2)}) collective-permute-start(f32[8,2,2,4]{3,2,1,0:T(2,128)} %pad_maximum_fusion.4), channel_id=1, source_target_pairs={{0,32},{16,48},{32,0},{48,16},{64,96},{80,112},{96,64},{112,80},{1... | collective-permute-start | bytes 1544 | tf_op jit(solution)/shard_map/ppermute | solution.py:292
  74.3 51.3 %collective-permute-start.7 = (f32[8,2,2,4]{3,2,1,0:T(2,128)}, f32[8,2,2,4]{3,2,1,0:T(2,128)S(1)}, u32[]{:S(2)}, u32[]{:S(2)}) collective-permute-start(f32[8,2,2,4]{3,2,1,0:T(2,128)} %pad_maximum_fusion.4), channel_id=1, source_target_pairs={{0,64},{16,80},{32,96},{48,112},{64,0},{80,16},{96,32},{112,48},{1... | collective-permute-start | bytes 1544 | tf_op jit(solution)/shard_map/ppermute | solution.py:292
  78.3 65.1 %collective-permute-start.8 = (f32[8,2,2,4]{3,2,1,0:T(2,128)}, f32[8,2,2,4]{3,2,1,0:T(2,128)S(1)}, u32[]{:S(2)}, u32[]{:S(2)}) collective-permute-start(f32[8,2,2,4]{3,2,1,0:T(2,128)} %pad_maximum_fusion.4), channel_id=1, source_target_pairs={{0,96},{16,112},{32,64},{48,80},{64,32},{80,48},{96,0},{112,16},{1... | collective-permute-start | bytes 1544 | tf_op jit(solution)/shard_map/ppermute | solution.py:292
  82.5 78.9 %collective-permute-start.11 = (bf16[4,512,128]{2,1,0:T(8,128)(2,1)}, bf16[4,512,128]{2,1,0:T(8,128)(2,1)S(1)}, u32[]{:S(2)}, u32[]{:S(2)}) collective-permute-start(bf16[4,512,128]{2,1,0:T(8,128)(2,1)} %get-tuple-element.33), channel_id=1, source_target_pairs={{0,3},{1,2},{2,1},{3,0},{4,7},{5,6},{6,5},{7,4},{8,11},{9,10},{10,... | collective-permute-start | bytes 1572872 | tf_op jit(solution)/shard_map/ppermute | solution.py:292
  90.3 71.1 %collective-permute-start.9 = (bf16[4,512,128]{2,1,0:T(8,128)(2,1)}, bf16[4,512,128]{2,1,0:T(8,128)(2,1)}, u32[]{:S(2)}, u32[]{:S(2)}) collective-permute-start(bf16[4,512,128]{2,1,0:T(8,128)(2,1)} %get-tuple-element.31), channel_id=1, source_target_pairs={{0,1},{1,0},{2,3},{3,2},{4,5},{5,4},{6,7},{7,6},{8,9},{9,8},{10,11... | collective-permute-start | bytes 1572872 | tf_op jit(solution)/shard_map/ppermute | solution.py:292
  143.6 60.4 %collective-permute-start.10 = (bf16[4,512,128]{2,1,0:T(8,128)(2,1)}, bf16[4,512,128]{2,1,0:T(8,128)(2,1)}, u32[]{:S(2)}, u32[]{:S(2)}) collective-permute-start(bf16[4,512,128]{2,1,0:T(8,128)(2,1)} %get-tuple-element.32), channel_id=1, source_target_pairs={{0,2},{1,3},{2,0},{3,1},{4,6},{5,7},{6,4},{7,5},{8,10},{9,11},{10,... | collective-permute-start | bytes 1572872 | tf_op jit(solution)/shard_map/ppermute | solution.py:292
